TPU v7x, 32 devices: a whole 2x2x4 slice. The times are simulated.
32 devices in a mesh: row: 8 (over y, x, core), col: 4 (over z).
Axes of the slice: x: 2, y: 2, z: 4, core: 2. Of those that a mesh axis runs over, the one named last changes fastest.
Arguments:
- images: bfloat16 [8, 32, 128, 256], P('row', 'col'), may hold values from -6 to 6
- weight: bfloat16 [3, 3, 256, 256], P(None, None, None, 'col'), may hold values from -0.125 to 0.125
- norm_gain: float32 [256], replicated, may hold values from 0.5 to 1.5
- cotangent: bfloat16 [8, 32, 128, 256], P('row', 'col'), may hold values from -6 to 6
Outputs:
- features: bfloat16 [8, 32, 128, 256], P('row', 'col')
- input_grad: bfloat16 [8, 32, 128, 256], P('row', 'col')
- weight_grad: float32 [3, 3, 256, 256], P(None, None, None, 'col')
All inputs are finite; a program needn't handle non-finite values.
Results may differ from a plain program's by a relative error of at most 0.013.
Values may be sent and summed in bfloat16 or wider, within the bound.
A program may use at most 64 MiB of HBM per device.

v0:
```python
import math

import jax
import jax.numpy as jnp
from jax import lax
from jax.sharding import PartitionSpec as P

epsilon = 1e-06
root_half = 0.7071067811865476
norm_const = 0.3989422804014327


def padded_2(value, sides, width):
    for axis, dim in sides:
        peers, length = (lax.axis_size(axis), value.shape[dim])
        up = [(i, (i + 1) % peers) for i in range(peers - 1)]
        down = [(j, i) for i, j in up]
        last = lax.slice_in_dim(value, length - width, length, axis=dim)
        initial = lax.slice_in_dim(value, 0, width, axis=dim)
        before = lax.ppermute(last, axis, up)
        after = lax.ppermute(initial, axis, down)
        value = jnp.concatenate([before, value, after], axis=dim)
    return value


def norm_act(conv_out, upper, norm_gain):
    mean_val = jnp.mean(conv_out, axis=-1, keepdims=True)
    centred = conv_out - mean_val
    variance = jnp.mean(centred * centred, axis=-1, keepdims=True)
    inv_std = lax.rsqrt(variance + epsilon)
    unit = centred * inv_std
    normed = unit * norm_gain
    cdf_val = 0.5 * (1.0 + lax.erf(normed * root_half))
    density = jnp.exp(-0.5 * normed * normed) * norm_const
    outputs = (normed * cdf_val).astype(jnp.bfloat16)
    upstream = upper.astype(jnp.float32) * (cdf_val + normed * density) * norm_gain
    mean_up = jnp.mean(upstream, axis=-1, keepdims=True)
    mean_cross = jnp.mean(upstream * unit, axis=-1, keepdims=True)
    grad_pre = inv_std * (upstream - mean_up - unit * mean_cross)
    return (outputs, grad_pre.astype(jnp.bfloat16))


def window(padded, tap_row, tap_col, tile_rows, tile_cols):
    return padded[:, tap_row : tap_row + tile_rows, tap_col : tap_col + tile_cols, :].reshape(
        -1, padded.shape[-1]
    )


def on_device(images, weight, norm_gain, cotangent):
    img_count, tile_rows, tile_cols, in_chan = images.shape
    whole_kernel = lax.all_gather(weight, "col", axis=3, tiled=True)
    out_chan = whole_kernel.shape[3]
    rimmed = padded_2(images, (("col", 1),), 1)
    padded = jnp.pad(rimmed, ((0, 0), (0, 0), (1, 1), (0, 0)))
    conv_out = jnp.zeros((img_count * tile_rows * tile_cols, out_chan), jnp.float32)
    for tap_row in range(3):
        for tap_col in range(3):
            conv_out = conv_out + jnp.dot(
                window(padded, tap_row, tap_col, tile_rows, tile_cols),
                whole_kernel[tap_row, tap_col],
                preferred_element_type=jnp.float32,
            )
    outputs, grad_pre = norm_act(conv_out, cotangent.reshape(-1, out_chan), norm_gain)
    grad_grid = grad_pre.reshape(img_count, tile_rows, tile_cols, out_chan)
    grad_rimmed = padded_2(grad_grid, (("col", 1),), 1)
    grad_pad = jnp.pad(grad_rimmed, ((0, 0), (0, 0), (1, 1), (0, 0)))
    grad_input = jnp.zeros((img_count * tile_rows * tile_cols, in_chan), jnp.float32)
    pieces = []
    for tap_row in range(3):
        for tap_col in range(3):
            grad_input = grad_input + lax.dot_general(
                window(grad_pad, 2 - tap_row, 2 - tap_col, tile_rows, tile_cols),
                whole_kernel[tap_row, tap_col],
                (((1,), (1,)), ((), ())),
                preferred_element_type=jnp.float32,
            )
            pieces.append(
                lax.dot_general(
                    window(padded, tap_row, tap_col, tile_rows, tile_cols),
                    grad_pre,
                    (((0,), (0,)), ((), ())),
                    preferred_element_type=jnp.float32,
                )
            )
    partial_value = jnp.stack(pieces).reshape(3, 3, in_chan, out_chan)
    totals = lax.psum(partial_value, ("row", "col"))
    col_share = out_chan // lax.axis_size("col")
    own_share = lax.dynamic_slice_in_dim(totals, lax.axis_index("col") * col_share, col_share, 3)
    pixels = img_count * lax.axis_size("row") * tile_rows * lax.axis_size("col") * tile_cols
    weight_grad = own_share * (1.0 / math.sqrt(pixels))
    features = outputs.reshape(img_count, tile_rows, tile_cols, out_chan)
    input_grad = grad_input.astype(jnp.bfloat16).reshape(img_count, tile_rows, tile_cols, in_chan)
    return (features, input_grad, weight_grad)


def solution(mesh):
    placed = (
        P("row", "col", None, None),
        P(None, None, None, "col"),
        P(),
        P("row", "col", None, None),
    )
    return jax.shard_map(
        on_device,
        mesh=mesh,
        in_specs=placed,
        out_specs=(
            P("row", "col", None, None),
            P("row", "col", None, None),
            P(None, None, None, "col"),
        ),
        check_vma=False,
    )
```

profile of v0, /device:TPU:0, one launch (start us, length us, event | category | flops | bytes accessed | tf_op | source)
XLA Modules:
  0.0 214.4 jit_solution(16011924250667744520)
XLA Ops:
  7.2 0.0 copy-start
  7.2 0.0 all-gather.2.cloned.1.call-start
  7.2 0.7 all-gather.2.cloned.1.call-update
  7.9 0.0 all-reduce.4.cloned.1.call-start
  8.0 0.9 fusion.29
  8.8 4.9 %collective-permute-start = (bf16[1,1,128,256]{3,2,1,0:T(8,128)(2,1)S(1)}, bf16[1,1,128,256]{3,2,1,0:T(8,128)(2,1)S(1)}, u32[]{:S(2)}, u32[]{:S(2)}) collective-permute-start(bf16[1,1,128,256]{3,2,1,0:T(8,128)(2,1)S(1)} %get-tuple-element.25), channel_id=1, source_target_pairs={{0,1},{1,2},{2,3},{4,5},{5,6},{6,7},{8,9},{9,10},{10,11},{12,13},{... | collective-permute-start | bytes 196616 | tf_op jit(solution)/shard_map/ppermute | solution.py:20
  13.8 1.3 collective-permute-start.1
  15.1 0.6 collective-permute-done
  15.7 4.3 %collective-permute-done.1 = bf16[1,1,128,256]{3,2,1,0:T(8,128)(2,1)S(1)} collective-permute-done((bf16[1,1,128,256]{3,2,1,0:T(8,128)(2,1)S(1)}, bf16[1,1,128,256]{3,2,1,0:T(8,128)(2,1)S(1)}, u32[]{:S(2)}, u32[]{:S(2)}) %collective-permute-start.1) | collective-permute-done | bytes 65568 | tf_op jit(solution)/shard_map/ppermute | solution.py:21
  19.9 1.3 select_maximum_fusion.2
  21.2 1.0 pad_maximum_fusion.2
  22.3 1.4 fusion.27
  23.6 19.1 %all-gather.2.cloned.1.call-done = bf16[3,3,256,256]{2,3,1,0:T(8,128)(2,1)} async-done(((bf16[3,3,256,64]{2,3,1,0:T(8,128)(2,1)}), bf16[3,3,256,256]{2,3,1,0:T(8,128)(2,1)}) %all-gather.2.cloned.1.call-update) | async-done | bytes 1179664 | tf_op jit(solution)/shard_map/all_gather | solution.py:51
  42.8 1.3 fusion.21
  44.1 0.3 fusion.23
  44.4 0.0 copy-start.6
  44.5 0.3 convolution_add_fusion.13
  44.8 0.0 copy-start.5
  44.8 0.7 copy-done.6
  45.5 0.3 convolution_add_fusion.12
  45.8 0.1 copy-done.5
  45.9 0.3 convolution_add_fusion.11
  46.2 0.0 copy-start.4
  46.2 0.3 convolution_add_fusion.10
  46.6 0.7 copy-done.4
  47.3 0.3 convolution_add_fusion.9
  47.6 0.3 convolution_add_fusion.8
  48.0 0.7 copy-done.7
  48.6 0.4 fusion.30
  49.1 0.0 copy-start.9
  49.1 0.4 multiply_reduce_fusion.1
  49.5 0.0 copy-done.10
  49.5 0.6 copy-done.9
  50.1 1.9 fusion.24
  52.0 0.8 multiply_convert_fusion
  52.9 1.0 fusion.12
  53.9 1.1 fusion.11
  55.0 1.1 fusion.10
  56.0 1.0 fusion.9
  57.1 1.0 fusion.8
  58.1 1.1 fusion.7
  59.2 1.0 fusion.6
  60.2 1.0 fusion.5
  61.3 2.9 %collective-permute-start.2 = (bf16[1,1,128,256]{3,2,1,0:T(8,128)(2,1)S(1)}, bf16[1,1,128,256]{3,2,1,0:T(8,128)(2,1)S(1)}, u32[]{:S(2)}, u32[]{:S(2)}) collective-permute-start(bf16[1,1,128,256]{3,2,1,0:T(8,128)(2,1)S(1)} %get-tuple-element.21), channel_id=1, source_target_pairs={{0,1},{1,2},{2,3},{4,5},{5,6},{6,7},{8,9},{9,10},{10,11},{12,13},{... | collective-permute-start | bytes 196616 | tf_op jit(solution)/shard_map/ppermute | solution.py:20
  64.2 1.3 collective-permute-start.3
  65.5 1.0 fusion.4
  66.5 3.1 %copy.8 = f32[3,3,256,256]{2,3,1,0:T(8,128)} copy(f32[3,3,256,256]{3,2,1,0:T(8,128)} %bitcast.40) | data formatting | bytes 4718592 | tf_op jit(solution)/shard_map/reshape | solution.py:85
  69.7 0.0 all-reduce.4.cloned.1.call-update
  69.7 0.0 collective-permute-done.2
  69.7 0.6 collective-permute-done.3
  70.3 0.2 select_maximum_fusion
  70.5 0.4 fusion.26
  70.9 0.1 pad_maximum_fusion
  71.0 0.3 fusion.20
  71.3 0.3 fusion.22
  71.6 0.3 convolution_add_fusion.6
  71.9 0.3 convolution_add_fusion.5
  72.2 0.3 convolution_add_fusion.4
  72.5 0.3 convolution_add_fusion.3
  72.8 0.3 convolution_add_fusion.2
  73.1 0.3 convolution_add_fusion.1
  73.4 1.1 fusion.3
  74.5 131.2 %all-reduce.4.cloned.1.call-done = f32[3,3,256,256]{2,3,1,0:T(8,128)} async-done(((f32[3,3,256,256]{2,3,1,0:T(8,128)}), f32[3,3,256,256]{2,3,1,0:T(8,128)}) %all-reduce.4.cloned.1.call-update) | async-done | bytes 2359312 | tf_op jit(solution)/shard_map/psum | solution.py:86
  205.7 1.9 dynamic-slice_multiply_fusion
  (15 shorter events, 0.0 us)
Async XLA Ops:
  7.2 14.1 %copy-start = (bf16[1,8,128,256]{3,2,1,0:T(8,128)(2,1)S(1)}, bf16[1,8,128,256]{3,2,1,0:T(8,128)(2,1)}, u32[]{:S(2)}) copy-start(bf16[1,8,128,256]{3,2,1,0:T(8,128)(2,1)} %param.4) | copy-start | bytes 1572868
  7.2 35.6 %all-gather.2.cloned.1.call-start = ((), (), s32[]{:S(2)}) async-start(), calls=%async_computation | async-start | bytes 1474560 | tf_op jit(solution)/shard_map/all_gather | solution.py:51
  7.9 197.8 %all-reduce.4.cloned.1.call-start = ((), (), s32[]{:S(2)}) async-start(), calls=%async_computation.1 | async-start | bytes 4718592 | tf_op jit(solution)/shard_map/psum | solution.py:86
  8.8 6.8 %collective-permute-start = (bf16[1,1,128,256]{3,2,1,0:T(8,128)(2,1)S(1)}, bf16[1,1,128,256]{3,2,1,0:T(8,128)(2,1)S(1)}, u32[]{:S(2)}, u32[]{:S(2)}) collective-permute-start(bf16[1,1,128,256]{3,2,1,0:T(8,128)(2,1)S(1)} %get-tuple-element.25), channel_id=1, source_target_pairs={{0,1},{1,2},{2,3},{4,5},{5,6},{6,7},{8,9},{9,10},{10,11},{12,13},{... | collective-permute-start | bytes 196616 | tf_op jit(solution)/shard_map/ppermute | solution.py:20
  13.8 6.2 %collective-permute-start.1 = (bf16[1,1,128,256]{3,2,1,0:T(8,128)(2,1)S(1)}, bf16[1,1,128,256]{3,2,1,0:T(8,128)(2,1)S(1)}, u32[]{:S(2)}, u32[]{:S(2)}) collective-permute-start(bf16[1,1,128,256]{3,2,1,0:T(8,128)(2,1)S(1)} %get-tuple-element.26), channel_id=1, source_target_pairs={{1,0},{2,1},{3,2},{5,4},{6,5},{7,6},{9,8},{10,9},{11,10},{13,12},{... | collective-permute-start | bytes 196616 | tf_op jit(solution)/shard_map/ppermute | solution.py:21
  23.6 24.0 %copy-start.2 = (bf16[1,8,128,256]{3,2,1,0:T(8,128)(2,1)}, bf16[1,8,128,256]{3,2,1,0:T(8,128)(2,1)S(1)}, u32[]{:S(2)}) copy-start(bf16[1,8,128,256]{3,2,1,0:T(8,128)(2,1)S(1)} %get-tuple-element.13) | copy-start | bytes 1572868
  42.8 1.4 copy-start.1
  42.8 1.7 copy-start.8
  44.4 1.0 copy-start.6
  44.8 1.1 copy-start.5
  46.2 1.0 copy-start.4
  47.6 1.0 copy-start.7
  48.6 0.8 copy-start.10
  49.1 1.0 copy-start.9
  57.1 2.1 copy-start.3
  61.3 8.4 %collective-permute-start.2 = (bf16[1,1,128,256]{3,2,1,0:T(8,128)(2,1)S(1)}, bf16[1,1,128,256]{3,2,1,0:T(8,128)(2,1)S(1)}, u32[]{:S(2)}, u32[]{:S(2)}) collective-permute-start(bf16[1,1,128,256]{3,2,1,0:T(8,128)(2,1)S(1)} %get-tuple-element.21), channel_id=1, source_target_pairs={{0,1},{1,2},{2,3},{4,5},{5,6},{6,7},{8,9},{9,10},{10,11},{12,13},{... | collective-permute-start | bytes 196616 | tf_op jit(solution)/shard_map/ppermute | solution.py:20
  64.2 6.2 %collective-permute-start.3 = (bf16[1,1,128,256]{3,2,1,0:T(8,128)(2,1)S(1)}, bf16[1,1,128,256]{3,2,1,0:T(8,128)(2,1)S(1)}, u32[]{:S(2)}, u32[]{:S(2)}) collective-permute-start(bf16[1,1,128,256]{3,2,1,0:T(8,128)(2,1)S(1)} %get-tuple-element.22), channel_id=1, source_target_pairs={{1,0},{2,1},{3,2},{5,4},{6,5},{7,6},{9,8},{10,9},{11,10},{13,12},{... | collective-permute-start | bytes 196616 | tf_op jit(solution)/shard_map/ppermute | solution.py:21
Sparse Core Ops, SparseCore 0:
  9.6 33.1 all-gather.1
  69.8 135.8 all-reduce.3
where the time goes:
time: 215 us; the launch traced here: 214 us
  waiting for transfers between devices  156 us (73%)
  matrix products  16.9 us (8%)
  between operations  14.3 us (7%)
  starting transfers between devices  10.5 us (5%)
  local copies, waits for them, and re-layouts  8.58 us (4%)
  other arithmetic  7.61 us (4%)
    psum x1, waiting for transfers between devices, on_device(): totals = lax.psum(partial_value, ('row', 'col'))  131 us
    all_gather x1, waiting for transfers between devices, on_device(): whole_kernel = lax.all_gather(weight, 'col', axis=3, tiled=True)  19.1 us
    dot_general x9, matrix products, on_device(): lax.dot_general(window(padded, tap_row, tap_col, tile_rows, tile_cols), g...  9.4 us
    ppermute x2, starting transfers between devices, padded_2(): before = lax.ppermute(last, axis, up)  7.85 us
    ppermute x2, waiting for transfers between devices, padded_2(): after = lax.ppermute(initial, axis, down)  4.91 us
  transfers between devices with their start and end apart: 6, of which 5 were waited for; matrix products, arithmetic and copies ran while one was open for 6% of the time, Pallas kernels for 0%

commit v1 on v0

v1 whole, which is shorter than its diff:
```python
import functools
import math

import jax
import jax.numpy as jnp
from jax import lax
from jax.experimental import pallas as pl
from jax.experimental.pallas import tpu as pltpu
from jax.sharding import PartitionSpec as P

epsilon = 1e-06
root_half = 0.7071067811865476
norm_const = 0.3989422804014327
MESH = pl.DeviceIdType.MESH
NT = (((1,), (1,)), ((), ()))


def norm_act(conv_out, upper, norm_gain):
    mean_val = jnp.mean(conv_out, axis=-1, keepdims=True)
    centred = conv_out - mean_val
    variance = jnp.mean(centred * centred, axis=-1, keepdims=True)
    inv_std = lax.rsqrt(variance + epsilon)
    unit = centred * inv_std
    normed = unit * norm_gain
    cdf_val = 0.5 * (1.0 + lax.erf(normed * root_half))
    density = jnp.exp(-0.5 * normed * normed) * norm_const
    outputs = (normed * cdf_val).astype(jnp.bfloat16)
    upstream = upper.astype(jnp.float32) * (cdf_val + normed * density) * norm_gain
    mean_up = jnp.mean(upstream, axis=-1, keepdims=True)
    mean_cross = jnp.mean(upstream * unit, axis=-1, keepdims=True)
    return (outputs, inv_std * (upstream - mean_up - unit * mean_cross))


def kernel(
    plan,
    x_ref,
    w_ref,
    gain_ref,
    cot_ref,
    feat_ref,
    igrad_ref,
    wg_ref,
    wt,
    x3,
    g3,
    gt,
    conv,
    x_halo,
    g_halo,
    parts,
    parts_in,
    gathered,
    z_in,
    *rest,
):
    rows, cols, quads, split, cs, rs = plan
    phases = quads.bit_length() - 1
    totals, totals_in = rest[: phases + 1], rest[phases + 1 : 2 * phases + 1]
    (halo_s, halo_r, wz_s, wz_r, wq_s, wq_r, sib_s, sib_r, ph_s, ph_r, z_s, z_r, ag_s, ag_r) = rest[
        2 * phases + 1 :
    ]
    tile_rows, width, chan = x_ref.shape
    out_chan = cs * cols
    taps = 3 * chan
    half_k = taps // 2
    half_w = 3 * half_k
    my_row, my_col = lax.axis_index("row"), lax.axis_index("col")
    quad, core = my_row // 2, my_row % 2
    sibling = (quad * 2 + 1 - core, my_col)
    bits, partners, partner_quads = [], [], []
    for j in range(phases):
        low, high = 1 << j, 1 << (phases - 1 - j)
        mask = low + core * (high - low)
        bit = (1 - core) * ((quad // low) % 2) + core * ((quad // high) % 2)
        other = quad + mask * (1 - 2 * bit)
        bits.append(bit)
        partner_quads.append(other)
        partners.append((other * 2 + core, my_col))
    started = []

    def send(src, dst, send_sem, recv_sem, device):
        copy = pltpu.make_async_remote_copy(
            src_ref=src,
            dst_ref=dst,
            send_sem=send_sem,
            recv_sem=recv_sem,
            device_id=device,
            device_id_type=MESH,
        )
        copy.start()
        started.append(copy)
        return copy

    def col_at(shift):
        return (my_col + cols + shift) % cols

    barrier = pltpu.get_barrier_semaphore()
    for d in range(1, rows):
        pl.semaphore_signal(
            barrier, inc=1, device_id=((my_row + d) % rows, my_col), device_id_type=MESH
        )
    for d in range(1, cols):
        pl.semaphore_signal(barrier, inc=1, device_id=(my_row, col_at(d)), device_id_type=MESH)

    eye = (
        lax.broadcasted_iota(jnp.int32, (cs, cs), 0) == lax.broadcasted_iota(jnp.int32, (cs, cs), 1)
    ).astype(jnp.bfloat16)
    own_rows = pl.ds(pl.multiple_of(my_col * cs, 16), cs)
    for k in range(3):
        wt[own_rows, k * taps : (k + 1) * taps] = lax.dot_general(
            eye, w_ref[k * taps : (k + 1) * taps, :], NT, preferred_element_type=jnp.float32
        ).astype(jnp.bfloat16)

    pl.semaphore_wait(barrier, rows + cols - 2)

    half_lanes = pl.ds(pl.multiple_of(core * half_w, 128), half_w)

    def piece(col, q):
        start = col * cs + (q * rs if split else 0)
        return wt.at[pl.ds(pl.multiple_of(start, 16), rs), half_lanes]

    wz = [None]
    for d in range(1, cols):
        own = piece(my_col, quad)
        wz.append(send(own, own, wz_s.at[d - 1], wz_r.at[d - 1], (my_row, col_at(d))))

    has_up, has_down = my_col > 0, my_col < cols - 1

    def halo_copies(first, last, into, base):
        up = pltpu.make_async_remote_copy(
            src_ref=first,
            dst_ref=into.at[1],
            send_sem=halo_s.at[base],
            recv_sem=halo_r.at[base],
            device_id=(my_row, col_at(-1)),
            device_id_type=MESH,
        )
        down = pltpu.make_async_remote_copy(
            src_ref=last,
            dst_ref=into.at[0],
            send_sem=halo_s.at[base + 1],
            recv_sem=halo_r.at[base + 1],
            device_id=(my_row, col_at(1)),
            device_id_type=MESH,
        )

        @pl.when(has_up)
        def _():
            up.start()

        @pl.when(has_down)
        def _():
            down.start()

        return up, down

    column = lax.broadcasted_iota(jnp.int32, (width, chan), 0)

    def spread(dst, row, value, flip):
        value = value.astype(jnp.float32)
        left = jnp.where(column == 0, 0.0, pltpu.roll(value, 1, 0))
        right = jnp.where(column == width - 1, 0.0, pltpu.roll(value, width - 1, 0))
        shifted = (right, value, left) if flip else (left, value, right)
        for c in range(3):
            dst[row, :, c * chan : (c + 1) * chan] = shifted[c].astype(jnp.bfloat16)

    def halo_rows(dst, into, copies, flip):
        up, down = copies

        @pl.when(has_up)
        def _():
            down.wait_recv()
            spread(dst, 0, into[0], flip)

        @pl.when(jnp.logical_not(has_up))
        def _():
            dst[0] = jnp.zeros(dst.shape[1:], dst.dtype)

        @pl.when(has_down)
        def _():
            up.wait_recv()
            spread(dst, tile_rows + 1, into[1], flip)

        @pl.when(jnp.logical_not(has_down))
        def _():
            dst[tile_rows + 1] = jnp.zeros(dst.shape[1:], dst.dtype)

    x_copies = halo_copies(x_ref.at[0], x_ref.at[tile_rows - 1], x_halo, 0)

    hops = {}
    if split:
        for d in range(1, cols):
            wz[d].wait_recv()
            got = piece(col_at(-d), quad)
            for j in range(2):
                hops[d, j] = send(got, got, wq_s.at[d - 1, j], wq_r.at[d - 1, j], partners[j])

    @pl.loop(0, tile_rows)
    def _(i):
        spread(x3, i + 1, x_ref[i], False)

    if split:
        for d in range(1, cols):
            hops[d, 0].wait_recv()
            got = piece(col_at(-d), partner_quads[0])
            hops[d, 2] = send(got, got, wq_s.at[d - 1, 2], wq_r.at[d - 1, 2], partners[1])
    halo_rows(x3, x_halo, x_copies, False)
    sib = []
    for d in range(1, cols):
        if split:
            hops[d, 1].wait_recv()
            hops[d, 2].wait_recv()
        else:
            wz[d].wait_recv()
        block = wt.at[pl.ds(pl.multiple_of(col_at(-d) * cs, 16), cs), half_lanes]
        sib.append(send(block, block, sib_s.at[d - 1], sib_r.at[d - 1], sibling))
    for copy in sib:
        copy.wait_recv()

    gain = gain_ref[...]
    half_rows = tile_rows // 2
    for b in range(2):
        acc = None
        for a in range(3):
            term = lax.dot_general(
                x3[b * half_rows + a : (b + 1) * half_rows + a].reshape(half_rows * width, taps),
                wt[:, a * taps : (a + 1) * taps],
                NT,
                preferred_element_type=jnp.float32,
            )
            acc = term if acc is None else acc + term
        conv[b * half_rows : (b + 1) * half_rows] = acc.reshape(half_rows, width, out_chan)

    @pl.loop(0, tile_rows)
    def _(i):
        outputs, grad_pre = norm_act(conv[i], cot_ref[i], gain)
        feat_ref[i] = outputs
        spread(g3, i + 1, grad_pre, True)
        gt[:, pl.ds(pl.multiple_of(i * width, 128), width)] = grad_pre.T.astype(jnp.bfloat16)

    centre = pl.ds(chan, chan)
    g_copies = halo_copies(g3.at[1, :, centre], g3.at[tile_rows, :, centre], g_halo, 2)

    def weight_part(k):
        acc = jnp.dot(
            gt[...],
            x3[k : k + tile_rows].reshape(tile_rows * width, taps),
            preferred_element_type=jnp.float32,
        ).astype(jnp.bfloat16)
        for h in range(2):
            for s in range(quads if split else 1):
                at = (s % 2) * 2 + s // 2 if split and h == 0 else s
                for c in range(cols):
                    first = c * cs + s * rs
                    parts[k, h, at, c] = acc[first : first + rs, h * half_k : (h + 1) * half_k]
        return send(
            parts.at[k, 1 - core], parts_in.at[k], ph_s.at[k, phases], ph_r.at[k, phases], sibling
        )

    def add(one, two):
        return (one.astype(jnp.float32) + two.astype(jnp.float32)).astype(jnp.bfloat16)

    def start_phase(k, j):
        size = totals_in[j].shape[1]
        source = totals[j].at[k, pl.ds((1 - bits[j]) * size, size)] if split else totals[j].at[k]
        return send(source, totals_in[j].at[k], ph_s.at[k, j], ph_r.at[k, j], partners[j])

    def after_siblings(k, copy):
        copy.wait_recv()
        totals[0][k] = add(parts[k, core], parts_in[k])
        return start_phase(k, 0)

    def after_phase(k, j, copy):
        copy.wait_recv()
        size = totals_in[j].shape[1]
        kept = totals[j][k, pl.ds(bits[j] * size, size)] if split else totals[j][k]
        totals[j + 1][k] = add(kept, totals_in[j][k])
        if j + 1 < phases:
            return start_phase(k, j + 1)
        return [
            send(
                totals[phases].at[k, 0, col_at(d)],
                z_in.at[k, d - 1],
                z_s.at[k, d - 1],
                z_r.at[k, d - 1],
                (my_row, col_at(d)),
            )
            for d in range(1, cols)
        ]

    at_quad = quad if split else 0

    def after_cols(k, copies):
        total = totals[phases][k, 0, my_col].astype(jnp.float32)
        for d, copy in enumerate(copies):
            copy.wait_recv()
            total = total + z_in[k, d].astype(jnp.float32)
        gathered[k, core, at_quad] = total.astype(jnp.bfloat16)
        if not split:
            return []
        own = gathered.at[k, core, quad]
        return [
            send(
                own, own, ag_s.at[k, d], ag_r.at[k, d], (((quad + d) % quads) * 2 + core, my_col)
            )
            for d in range(1, quads)
        ]

    def after_quads(k, copies):
        for copy in copies:
            copy.wait_recv()
        own = gathered.at[k, core]
        return send(own, own, ag_s.at[k, 0], ag_r.at[k, 0], sibling)

    scale = 1.0 / math.sqrt(tile_rows * width * rows * cols)

    def finish(k, copy):
        copy.wait_recv()
        for h in range(2):
            first = k * taps + h * half_k
            wg_ref[:, first : first + half_k] = (
                gathered[k, h].astype(jnp.float32).reshape(cs, half_k) * scale
            )

    quarter = tile_rows // 4

    def input_part(b):
        acc = None
        for a in range(3):
            for c in range(3):
                first = b * quarter + 2 - a
                term = jnp.dot(
                    g3[first : first + quarter, :, c * chan : (c + 1) * chan].reshape(
                        quarter * width, out_chan
                    ),
                    wt[:, a * taps + c * chan : a * taps + (c + 1) * chan],
                    preferred_element_type=jnp.float32,
                )
                acc = term if acc is None else acc + term
        igrad_ref[b * quarter : (b + 1) * quarter] = acc.astype(jnp.bfloat16).reshape(
            quarter, width, chan
        )

    flight = [None] * 3
    flight[0] = weight_part(0)
    flight[1] = weight_part(1)
    flight[0] = after_siblings(0, flight[0])
    flight[2] = weight_part(2)
    flight[1] = after_siblings(1, flight[1])
    input_part(1)
    flight[2] = after_siblings(2, flight[2])
    for j in range(phases):
        for k in range(3):
            flight[k] = after_phase(k, j, flight[k])
        if j == 0:
            input_part(2)
    halo_rows(g3, g_halo, g_copies, True)
    input_part(0)
    for k in range(3):
        flight[k] = after_cols(k, flight[k])
    input_part(3)
    for k in range(3):
        flight[k] = after_quads(k, flight[k])
    for k in range(3):
        finish(k, flight[k])

    for copy in started:
        copy.wait_send()
    for up, down in (x_copies, g_copies):

        @pl.when(has_up)
        def _():
            up.wait_send()

        @pl.when(has_down)
        def _():
            down.wait_send()


def on_device(images, weight, norm_gain, cotangent):
    _, tile_rows, width, chan = images.shape
    rows, cols = lax.axis_size("row"), lax.axis_size("col")
    cs = weight.shape[3]
    quads = rows // 2
    split = quads == 4 and cs % 64 == 0
    pieces = quads if split else 1
    rs = cs // pieces
    phases = quads.bit_length() - 1
    out_chan = cs * cols
    taps = 3 * chan
    half = taps // 2
    bf16 = jnp.bfloat16
    vmem = pltpu.VMEM
    dma = pltpu.SemaphoreType.DMA
    counts = [pieces >> j if split else 1 for j in range(phases + 1)]
    scratch = [
        vmem((out_chan, 3 * taps), bf16),
        vmem((tile_rows + 2, width, taps), bf16),
        vmem((tile_rows + 2, width, 3 * out_chan), bf16),
        vmem((out_chan, tile_rows * width), bf16),
        vmem((tile_rows, width, out_chan), jnp.float32),
        vmem((2, width, chan), bf16),
        vmem((2, width, out_chan), bf16),
        vmem((3, 2, pieces, cols, rs, half), bf16),
        vmem((3, pieces, cols, rs, half), bf16),
        vmem((3, 2, pieces, rs, half), bf16),
        vmem((3, cols - 1, rs, half), bf16),
    ]
    scratch += [vmem((3, n, cols, rs, half), bf16) for n in counts]
    scratch += [vmem((3, n, cols, rs, half), bf16) for n in counts[1:]]
    for shape in (
        (4,),
        (cols - 1,),
        (cols - 1, 3),
        (cols - 1,),
        (3, phases + 1),
        (3, cols - 1),
        (3, quads),
    ):
        scratch += [dma(shape), dma(shape)]
    in_vmem = pl.BlockSpec(memory_space=pltpu.VMEM)
    flops = 3 * 2 * tile_rows * width * 3 * taps * out_chan
    features, input_grad, wide_grad = pl.pallas_call(
        functools.partial(kernel, (rows, cols, quads, split, cs, rs)),
        out_shape=(
            jax.ShapeDtypeStruct((tile_rows, width, out_chan), bf16),
            jax.ShapeDtypeStruct((tile_rows, width, chan), bf16),
            jax.ShapeDtypeStruct((cs, 3 * taps), jnp.float32),
        ),
        in_specs=[in_vmem] * 4,
        out_specs=(in_vmem,) * 3,
        scratch_shapes=scratch,
        cost_estimate=pl.CostEstimate(
            flops=flops, bytes_accessed=4 << 20, transcendentals=2 * tile_rows * width * out_chan
        ),
        compiler_params=pltpu.CompilerParams(
            collective_id=0, has_side_effects=True, vmem_limit_bytes=48 << 20
        ),
    )(
        images.reshape(tile_rows, width, chan),
        weight.reshape(3 * taps, cs),
        norm_gain.reshape(1, out_chan),
        cotangent.reshape(tile_rows, width, out_chan),
    )
    weight_grad = wide_grad.T.reshape(3, 3, chan, cs)
    return (features[None], input_grad[None], weight_grad)


def solution(mesh):
    placed = (
        P("row", "col", None, None),
        P(None, None, None, "col"),
        P(),
        P("row", "col", None, None),
    )
    return jax.shard_map(
        on_device,
        mesh=mesh,
        in_specs=placed,
        out_specs=(
            P("row", "col", None, None),
            P("row", "col", None, None),
            P(None, None, None, "col"),
        ),
        check_vma=False,
    )
```

time: 215 us -> 50.5 us (0.23)
  waiting for transfers between devices: 156 us -> 0 us
  Pallas kernels: 0 us -> 43.7 us
  matrix products: 16.9 us -> 0 us
  between operations: 14.3 us -> 0.68 us
  starting transfers between devices: 10.5 us -> 0 us
  other arithmetic: 7.61 us -> 0 us
  local copies, waits for them, and re-layouts: 8.58 us -> 5.87 us
    psum x1 -> x0, waiting for transfers between devices: 131 us -> none  [on_device(): totals = lax.psum(partial_value, ('row', 'col'))]
    pallas_call x0 -> x1, Pallas kernels: none -> 43.7 us  [on_device(): pl.pallas_call(functools.partial(kernel, (rows, cols, quads, split, cs, r...]
    all_gather x1 -> x0, waiting for transfers between devices: 19.1 us -> none  [on_device(): whole_kernel = lax.all_gather(weight, 'col', axis=3, tiled=True)]
    dot_general x27 -> x0, matrix products: 16.9 us -> none  [the longest x9 9.4 us: on_device(): lax.dot_general(window(padded, tap_row, tap_col, tile_rows, tile_cols), g...]
    ppermute x4 -> x0, starting transfers between devices: 10.4 us -> none  [the longest x2 7.85 us: padded_2(): before = lax.ppermute(last, axis, up)]
    ppermute x4 -> x0, waiting for transfers between devices: 5.5 us -> none  [the longest x2 4.91 us: padded_2(): after = lax.ppermute(initial, axis, down)]
    reshape x1, local copies, waits for them, and re-layouts: 3.14 us -> 0.31 us  [on_device(): weight_grad = wide_grad.T.reshape(3, 3, chan, cs)]
    unnamed x22 -> x10, local copies, waits for them, and re-layouts: 2.8 us -> 5.55 us
  transfers between devices with their start and end apart: 6 -> 0, of which waited for: 5 -> 0; matrix products, arithmetic and copies ran while one was open for 6% -> 0% of each run, Pallas kernels for 0% -> 0%
where the time goes in v1:
time: 50.5 us; the launch traced here: 50.3 us
  Pallas kernels  43.7 us (87%)
  local copies, waits for them, and re-layouts  5.87 us (12%)
  between operations  0.68 us (1%)
    pallas_call x1, Pallas kernels, on_device(): pl.pallas_call(functools.partial(kernel, (rows, cols, quads, split, cs, r...  43.7 us
    unnamed x10, local copies, waits for them, and re-layouts  5.55 us

profile of v1, /device:TPU:0, one launch (start us, length us, event | category | flops | bytes accessed | tf_op | source)
XLA Modules:
  0.0 50.3 jit_solution(14120362658353082009)
XLA Ops:
  0.6 0.0 copy-start
  0.6 1.3 %copy.9 = bf16[3,3,256,64]{3,2,1,0:T(8,128)(2,1)S(1)} copy(bf16[3,3,256,64]{2,3,1,0:T(8,128)(2,1)} %param.5) | data formatting | bytes 589824 | tf_op args[1]
  2.0 0.0 copy-start.2
  2.0 0.0 copy-done
  2.0 0.7 %copy-done.2 = f32[256]{0:T(256)S(1)} copy-done((f32[256]{0:T(256)S(1)}, f32[256]{0:T(256)}, u32[]{:S(2)}) %copy-start.2) | copy-done | bytes 1048
  2.7 0.0 copy-start.1
  2.7 1.0 %copy-done.1 = bf16[1,8,128,256]{3,2,1,0:T(8,128)(2,1)S(1)} copy-done((bf16[1,8,128,256]{3,2,1,0:T(8,128)(2,1)S(1)}, bf16[1,8,128,256]{3,2,1,0:T(8,128)(2,1)}, u32[]{:S(2)}) %copy-start.1) | copy-done | bytes 524312
  3.7 43.7 %shard_map.67 = (bf16[8,128,256]{2,1,0:T(8,128)(2,1)S(1)}, bf16[8,128,256]{2,1,0:T(8,128)(2,1)S(1)}, f32[64,2304]{1,0:T(8,128)S(1)}) custom-call(bf16[8,128,256]{2,1,0:T(8,128)(2,1)S(1)} %bitcast.13, bf16[2304,64]{1,0:T(8,128)(2,1)S(1)} %bitcast.9, f32[1,256]{1,0:T(1,128)S(1)} %bitcast.15, bf16[8,128,256]{2,1,0:T(8,128)(2,1)S(1)} %bitcast.14), custom_call_target="tpu_custom_call" | custom-call | flops 3623878656 | bytes 4194304 | tf_op jit(solution)/shard_map/pallas_call | solution.py:423
  47.4 0.3 reshape.25
  47.8 0.9 %copy.10 = f32[3,3,256,64]{2,3,1,0:T(8,128)} copy(f32[3,3,256,64]{2,1,0,3:T(4,128)S(1)} %reshape.25) | data formatting | bytes 1179648
  48.7 0.8 %copy.13 = bf16[1,8,128,256]{3,2,1,0:T(8,128)(2,1)} copy(bf16[1,8,128,256]{3,2,1,0:T(8,128)(2,1)S(1)} %bitcast.12) | data formatting | bytes 1048576
  49.5 0.8 %copy.14 = bf16[1,8,128,256]{3,2,1,0:T(8,128)(2,1)} copy(bf16[1,8,128,256]{3,2,1,0:T(8,128)(2,1)S(1)} %bitcast.11) | data formatting | bytes 1048576
Async XLA Ops:
  0.6 1.4 %copy-start = (bf16[1,8,128,256]{3,2,1,0:T(8,128)(2,1)S(1)}, bf16[1,8,128,256]{3,2,1,0:T(8,128)(2,1)}, u32[]{:S(2)}) copy-start(bf16[1,8,128,256]{3,2,1,0:T(8,128)(2,1)} %param.4) | copy-start | bytes 1572868
  2.0 0.7 %copy-start.2 = (f32[256]{0:T(256)S(1)}, f32[256]{0:T(256)}, u32[]{:S(2)}) copy-start(f32[256]{0:T(256)} %param.6) | copy-start | bytes 3076
  2.7 1.0 %copy-start.1 = (bf16[1,8,128,256]{3,2,1,0:T(8,128)(2,1)S(1)}, bf16[1,8,128,256]{3,2,1,0:T(8,128)(2,1)}, u32[]{:S(2)}) copy-start(bf16[1,8,128,256]{3,2,1,0:T(8,128)(2,1)} %param.7) | copy-start | bytes 1572868

commit v2 on v1

--- a/solution.py
+++ b/solution.py
@@ -44,7 +44,14 @@
     x3,
     g3,
     gt,
-    conv,
+    conv_even,
+    conv_odd,
+    g_pad,
+    x_own,
+    cot_own,
+    feat_own,
+    igrad_own,
+    wg_own,
     x_halo,
     g_halo,
     parts,
@@ -56,7 +63,7 @@
     rows, cols, quads, split, cs, rs = plan
     phases = quads.bit_length() - 1
     totals, totals_in = rest[: phases + 1], rest[phases + 1 : 2 * phases + 1]
-    (halo_s, halo_r, wz_s, wz_r, wq_s, wq_r, sib_s, sib_r, ph_s, ph_r, z_s, z_r, ag_s, ag_r) = rest[
+    (in_sem, out_sem, halo_s, halo_r, wz_s, wz_r, wq_s, wq_r, sib_s, sib_r, ph_s, ph_r, z_s, z_r, ag_s, ag_r) = rest[
         2 * phases + 1 :
     ]
     tile_rows, width, chan = x_ref.shape
@@ -102,14 +109,20 @@
     for d in range(1, cols):
         pl.semaphore_signal(barrier, inc=1, device_id=(my_row, col_at(d)), device_id_type=MESH)
 
-    eye = (
-        lax.broadcasted_iota(jnp.int32, (cs, cs), 0) == lax.broadcasted_iota(jnp.int32, (cs, cs), 1)
-    ).astype(jnp.bfloat16)
     own_rows = pl.ds(pl.multiple_of(my_col * cs, 16), cs)
-    for k in range(3):
-        wt[own_rows, k * taps : (k + 1) * taps] = lax.dot_general(
-            eye, w_ref[k * taps : (k + 1) * taps, :], NT, preferred_element_type=jnp.float32
-        ).astype(jnp.bfloat16)
+    own_copies = []
+    for t in range(9):
+        own_copies.append(
+            pltpu.make_async_copy(
+                w_ref.at[t], wt.at[own_rows, t * chan : (t + 1) * chan], in_sem.at[t]
+            )
+        )
+    x_copy = pltpu.make_async_copy(x_ref, x_own, in_sem.at[9])
+    cot_copy = pltpu.make_async_copy(cot_ref, cot_own, in_sem.at[10])
+    for copy in own_copies + [x_copy, cot_copy]:
+        copy.start()
+    for copy in own_copies:
+        copy.wait()
 
     pl.semaphore_wait(barrier, rows + cols - 2)
 
@@ -195,9 +208,11 @@
             for j in range(2):
                 hops[d, j] = send(got, got, wq_s.at[d - 1, j], wq_r.at[d - 1, j], partners[j])
 
+    x_copy.wait()
+
     @pl.loop(0, tile_rows)
     def _(i):
-        spread(x3, i + 1, x_ref[i], False)
+        spread(x3, i + 1, x_own[i], False)
 
     if split:
         for d in range(1, cols):
@@ -218,25 +233,48 @@
         copy.wait_recv()
 
     gain = gain_ref[...]
-    half_rows = tile_rows // 2
-    for b in range(2):
+    quarter = tile_rows // 4
+    strip = 32
+
+    def convolve(b, into):
         acc = None
         for a in range(3):
             term = lax.dot_general(
-                x3[b * half_rows + a : (b + 1) * half_rows + a].reshape(half_rows * width, taps),
+                x3[pl.ds(b * quarter + a, quarter)].reshape(quarter * width, taps),
                 wt[:, a * taps : (a + 1) * taps],
                 NT,
                 preferred_element_type=jnp.float32,
             )
             acc = term if acc is None else acc + term
-        conv[b * half_rows : (b + 1) * half_rows] = acc.reshape(half_rows, width, out_chan)
-
-    @pl.loop(0, tile_rows)
-    def _(i):
-        outputs, grad_pre = norm_act(conv[i], cot_ref[i], gain)
-        feat_ref[i] = outputs
-        spread(g3, i + 1, grad_pre, True)
-        gt[:, pl.ds(pl.multiple_of(i * width, 128), width)] = grad_pre.T.astype(jnp.bfloat16)
+        into[...] = acc.reshape(quarter, width, out_chan)
+
+    def act(b, source):
+        for r in range(quarter):
+            i = b * quarter + r
+            for first in range(0, width, strip):
+                span = slice(first, first + strip)
+                outputs, grad_pre = norm_act(source[r, span], cot_own[i, span], gain)
+                feat_own[i, span] = outputs
+                g_pad[r, 8 + first : 8 + first + strip] = grad_pre
+            value = g_pad[r, 8 : 8 + width].astype(jnp.bfloat16)
+            g3[i + 1, :, 0:out_chan] = g_pad[r, 9 : 9 + width].astype(jnp.bfloat16)
+            g3[i + 1, :, out_chan : 2 * out_chan] = value
+            g3[i + 1, :, 2 * out_chan :] = g_pad[r, 7 : 7 + width].astype(jnp.bfloat16)
+            gt[:, pl.ds(pl.multiple_of(i * width, 128), width)] = value.T
+
+    g_pad[...] = jnp.zeros(g_pad.shape, g_pad.dtype)
+    cot_copy.wait()
+    convolve(0, conv_even)
+
+    @pl.loop(0, 2)
+    def _(t):
+        convolve(2 * t + 1, conv_odd)
+        act(2 * t, conv_even)
+        convolve(jnp.minimum(2 * t + 2, 3), conv_even)
+        act(2 * t + 1, conv_odd)
+
+    feat_copy = pltpu.make_async_copy(feat_own, feat_ref, out_sem.at[0])
+    feat_copy.start()
 
     centre = pl.ds(chan, chan)
     g_copies = halo_copies(g3.at[1, :, centre], g3.at[tile_rows, :, centre], g_halo, 2)
@@ -317,12 +355,15 @@
     def finish(k, copy):
         copy.wait_recv()
         for h in range(2):
-            first = k * taps + h * half_k
-            wg_ref[:, first : first + half_k] = (
-                gathered[k, h].astype(jnp.float32).reshape(cs, half_k) * scale
-            )
-
-    quarter = tile_rows // 4
+            value = gathered[k, h].astype(jnp.float32).reshape(cs, half_k) * scale
+            for lane in range(0, half_k, 128):
+                tap, at = divmod(h * half_k + lane, chan)
+                wg_own[3 * k + tap, :, at : at + 128] = value[:, lane : lane + 128]
+        done = pltpu.make_async_copy(
+            wg_own.at[3 * k : 3 * k + 3], wg_ref.at[3 * k : 3 * k + 3], out_sem.at[2 + k]
+        )
+        done.start()
+        return done
 
     def input_part(b):
         acc = None
@@ -337,7 +378,7 @@
                     preferred_element_type=jnp.float32,
                 )
                 acc = term if acc is None else acc + term
-        igrad_ref[b * quarter : (b + 1) * quarter] = acc.astype(jnp.bfloat16).reshape(
+        igrad_own[b * quarter : (b + 1) * quarter] = acc.astype(jnp.bfloat16).reshape(
             quarter, width, chan
         )
 
@@ -359,13 +400,17 @@
     for k in range(3):
         flight[k] = after_cols(k, flight[k])
     input_part(3)
+    igrad_copy = pltpu.make_async_copy(igrad_own, igrad_ref, out_sem.at[1])
+    igrad_copy.start()
     for k in range(3):
         flight[k] = after_quads(k, flight[k])
     for k in range(3):
-        finish(k, flight[k])
+        flight[k] = finish(k, flight[k])
 
     for copy in started:
         copy.wait_send()
+    for copy in [feat_copy, igrad_copy] + flight:
+        copy.wait()
     for up, down in (x_copies, g_copies):
 
         @pl.when(has_up)
@@ -375,6 +420,17 @@
         @pl.when(has_down)
         def _():
             down.wait_send()
+
+
+def move(*refs):
+    count = len(refs) // 2
+    copies = [
+        pltpu.make_async_copy(refs[i], refs[count + i], refs[-1].at[i]) for i in range(count)
+    ]
+    for copy in copies:
+        copy.start()
+    for copy in copies:
+        copy.wait()
 
 
 def on_device(images, weight, norm_gain, cotangent):
@@ -398,7 +454,14 @@
         vmem((tile_rows + 2, width, taps), bf16),
         vmem((tile_rows + 2, width, 3 * out_chan), bf16),
         vmem((out_chan, tile_rows * width), bf16),
-        vmem((tile_rows, width, out_chan), jnp.float32),
+        vmem((tile_rows // 4, width, out_chan), jnp.float32),
+        vmem((tile_rows // 4, width, out_chan), jnp.float32),
+        vmem((tile_rows // 4, width + 16, out_chan), jnp.float32),
+        vmem((tile_rows, width, chan), bf16),
+        vmem((tile_rows, width, out_chan), bf16),
+        vmem((tile_rows, width, out_chan), bf16),
+        vmem((tile_rows, width, chan), bf16),
+        vmem((9, cs, chan), jnp.float32),
         vmem((2, width, chan), bf16),
         vmem((2, width, out_chan), bf16),
         vmem((3, 2, pieces, cols, rs, half), bf16),
@@ -408,6 +471,7 @@
     ]
     scratch += [vmem((3, n, cols, rs, half), bf16) for n in counts]
     scratch += [vmem((3, n, cols, rs, half), bf16) for n in counts[1:]]
+    scratch += [dma((11,)), dma((5,))]
     for shape in (
         (4,),
         (cols - 1,),
@@ -418,31 +482,40 @@
         (3, quads),
     ):
         scratch += [dma(shape), dma(shape)]
-    in_vmem = pl.BlockSpec(memory_space=pltpu.VMEM)
+    anywhere = pl.BlockSpec(memory_space=pl.ANY)
     flops = 3 * 2 * tile_rows * width * 3 * taps * out_chan
-    features, input_grad, wide_grad = pl.pallas_call(
+    shapes = (
+        jax.ShapeDtypeStruct((tile_rows, width, out_chan), bf16),
+        jax.ShapeDtypeStruct((tile_rows, width, chan), bf16),
+        jax.ShapeDtypeStruct((9, cs, chan), jnp.float32),
+    )
+    results = pl.pallas_call(
         functools.partial(kernel, (rows, cols, quads, split, cs, rs)),
-        out_shape=(
-            jax.ShapeDtypeStruct((tile_rows, width, out_chan), bf16),
-            jax.ShapeDtypeStruct((tile_rows, width, chan), bf16),
-            jax.ShapeDtypeStruct((cs, 3 * taps), jnp.float32),
-        ),
-        in_specs=[in_vmem] * 4,
-        out_specs=(in_vmem,) * 3,
+        out_shape=shapes,
+        in_specs=[anywhere, anywhere, pl.BlockSpec(memory_space=pltpu.VMEM), anywhere],
+        out_specs=(anywhere,) * 3,
         scratch_shapes=scratch,
         cost_estimate=pl.CostEstimate(
             flops=flops, bytes_accessed=4 << 20, transcendentals=2 * tile_rows * width * out_chan
         ),
         compiler_params=pltpu.CompilerParams(
-            collective_id=0, has_side_effects=True, vmem_limit_bytes=48 << 20
+            collective_id=0, has_side_effects=True, vmem_limit_bytes=60 << 20
         ),
     )(
         images.reshape(tile_rows, width, chan),
-        weight.reshape(3 * taps, cs),
+        jnp.swapaxes(weight, 2, 3).reshape(9, cs, chan),
         norm_gain.reshape(1, out_chan),
         cotangent.reshape(tile_rows, width, out_chan),
     )
-    weight_grad = wide_grad.T.reshape(3, 3, chan, cs)
+    features, input_grad, wide_grad = pl.pallas_call(
+        move,
+        out_shape=shapes,
+        in_specs=[anywhere] * 3,
+        out_specs=(anywhere,) * 3,
+        scratch_shapes=[dma((3,))],
+        compiler_params=pltpu.CompilerParams(vmem_limit_bytes=60 << 20),
+    )(*results)
+    weight_grad = jnp.swapaxes(wide_grad.reshape(3, 3, cs, chan), 2, 3)
     return (features[None], input_grad[None], weight_grad)
 
 

time: 50.5 us -> 94.9 us (1.88)
  Pallas kernels: 43.7 us -> 93.5 us
  local copies, waits for them, and re-layouts: 5.87 us -> 0 us
    pallas_call x0 -> x1, Pallas kernels: none -> 50.8 us  [on_device(): pl.pallas_call(move, out_shape=shapes, in_specs=[anywhere] * 3, out_specs...]
    unnamed x10 -> x0, local copies, waits for them, and re-layouts: 5.55 us -> none
    pallas_call x1, Pallas kernels: 43.7 us -> 42.8 us  [on_device(): pl.pallas_call(functools.partial(kernel, (rows, cols, quads, split, cs, r...]
where the time goes in v2:
time: 94.9 us; the launch traced here: 94.2 us
  Pallas kernels  93.5 us (99%)
    pallas_call x1, Pallas kernels, on_device(): pl.pallas_call(move, out_shape=shapes, in_specs=[anywhere] * 3, out_specs...  50.8 us
    pallas_call x1, Pallas kernels, on_device(): pl.pallas_call(functools.partial(kernel, (rows, cols, quads, split, cs, r...  42.8 us

profile of v2, /device:TPU:0, one launch (start us, length us, event | category | flops | bytes accessed | tf_op | source)
XLA Modules:
  0.0 94.2 jit_solution(11510467866248290969)
XLA Ops:
  0.6 42.8 %shard_map.67 = (bf16[8,128,256]{2,1,0:T(8,128)(2,1)}, bf16[8,128,256]{2,1,0:T(8,128)(2,1)}, f32[9,64,256]{2,1,0:T(8,128)}) custom-call(bf16[8,128,256]{2,1,0:T(8,128)(2,1)} %bitcast.12, bf16[9,64,256]{2,1,0:T(8,128)(2,1)} %bitcast.16, f32[1,256]{1,0:T(1,128)} %bitcast.17, bf16[8,128,256]{2,1,0:T(8,128)(2,1)} %bitcast.13), custom_call_target="tpu_custom_call" | custom-call | flops 3623878656 | bytes 4194304 | tf_op jit(solution)/shard_map/pallas_call | solution.py:492
  43.4 50.8 %shard_map.68 = (bf16[8,128,256]{2,1,0:T(8,128)(2,1)}, bf16[8,128,256]{2,1,0:T(8,128)(2,1)}, f32[9,64,256]{2,1,0:T(8,128)}) custom-call(bf16[8,128,256]{2,1,0:T(8,128)(2,1)} %get-tuple-element.9.refs_0_, bf16[8,128,256]{2,1,0:T(8,128)(2,1)} %get-tuple-element.10.refs_1_, f32[9,64,256]{2,1,0:T(8,128)} %get-tuple-element.11.refs_2_), custom_call_target="tpu_custom_call" | custom-call | tf_op jit(solution)/shard_map/pallas_call | solution.py:510

commit v3 on v2

--- a/solution.py
+++ b/solution.py
@@ -37,9 +37,9 @@
     w_ref,
     gain_ref,
     cot_ref,
-    feat_ref,
-    igrad_ref,
-    wg_ref,
+    feat_own,
+    igrad_own,
+    wg_own,
     wt,
     x3,
     g3,
@@ -49,9 +49,6 @@
     g_pad,
     x_own,
     cot_own,
-    feat_own,
-    igrad_own,
-    wg_own,
     x_halo,
     g_halo,
     parts,
@@ -63,7 +60,7 @@
     rows, cols, quads, split, cs, rs = plan
     phases = quads.bit_length() - 1
     totals, totals_in = rest[: phases + 1], rest[phases + 1 : 2 * phases + 1]
-    (in_sem, out_sem, halo_s, halo_r, wz_s, wz_r, wq_s, wq_r, sib_s, sib_r, ph_s, ph_r, z_s, z_r, ag_s, ag_r) = rest[
+    (in_sem, halo_s, halo_r, wz_s, wz_r, wq_s, wq_r, sib_s, sib_r, ph_s, ph_r, z_s, z_r, ag_s, ag_r, all_s, all_r) = rest[
         2 * phases + 1 :
     ]
     tile_rows, width, chan = x_ref.shape
@@ -132,10 +129,33 @@
         start = col * cs + (q * rs if split else 0)
         return wt.at[pl.ds(pl.multiple_of(start, 16), rs), half_lanes]
 
-    wz = [None]
-    for d in range(1, cols):
-        own = piece(my_col, quad)
-        wz.append(send(own, own, wz_s.at[d - 1], wz_r.at[d - 1], (my_row, col_at(d))))
+    def other_col(e):
+        first = e + (cols + e - my_col) // cols
+        last = cols - 1 - (e + (e + 1 + my_col) // cols)
+        far = (2 * my_col) // cols
+        return first + far * (last - first)
+
+    own = piece(my_col, quad)
+    wz = []
+    for e in range(cols - 1):
+        to = other_col(e)
+        wz.append(
+            pltpu.make_async_remote_copy(
+                src_ref=own,
+                dst_ref=own,
+                send_sem=wz_s.at[to],
+                recv_sem=wz_r.at[my_col],
+                device_id=(my_row, to),
+                device_id_type=MESH,
+            )
+        )
+        wz[e].start()
+
+    def arrived(e):
+        col = other_col(e)
+        got = piece(col, quad)
+        pltpu.make_async_copy(got, got, wz_r.at[col]).wait()
+        return col, got
 
     has_up, has_down = my_col > 0, my_col < cols - 1
 
@@ -201,34 +221,57 @@
     x_copies = halo_copies(x_ref.at[0], x_ref.at[tile_rows - 1], x_halo, 0)
 
     hops = {}
+
+    def pass_on(e):
+        col, got = arrived(e)
+        for j in range(2):
+            hops[e, j] = send(got, got, wq_s.at[e, j], wq_r.at[e, j], partners[j])
+
+    def pass_again(e):
+        hops[e, 0].wait_recv()
+        got = piece(other_col(e), partner_quads[0])
+        hops[e, 2] = send(got, got, wq_s.at[e, 2], wq_r.at[e, 2], partners[1])
+
+    sib = []
+
+    def to_sibling(e):
+        if split:
+            hops[e, 1].wait_recv()
+            hops[e, 2].wait_recv()
+            col = other_col(e)
+        else:
+            col, _ = arrived(e)
+        block = wt.at[pl.ds(pl.multiple_of(col * cs, 16), cs), half_lanes]
+        sib.append(send(block, block, sib_s.at[e], sib_r.at[e], sibling))
+
+    def spread_rows(first, last):
+        @pl.loop(first, last)
+        def _(i):
+            spread(x3, i + 1, x_own[i], False)
+
+    x_copy.wait()
+    steps = cols - 1
+    cut = tile_rows // 4
+    spread_rows(0, cut)
     if split:
-        for d in range(1, cols):
-            wz[d].wait_recv()
-            got = piece(col_at(-d), quad)
-            for j in range(2):
-                hops[d, j] = send(got, got, wq_s.at[d - 1, j], wq_r.at[d - 1, j], partners[j])
-
-    x_copy.wait()
-
-    @pl.loop(0, tile_rows)
-    def _(i):
-        spread(x3, i + 1, x_own[i], False)
-
-    if split:
-        for d in range(1, cols):
-            hops[d, 0].wait_recv()
-            got = piece(col_at(-d), partner_quads[0])
-            hops[d, 2] = send(got, got, wq_s.at[d - 1, 2], wq_r.at[d - 1, 2], partners[1])
-    halo_rows(x3, x_halo, x_copies, False)
-    sib = []
-    for d in range(1, cols):
-        if split:
-            hops[d, 1].wait_recv()
-            hops[d, 2].wait_recv()
-        else:
-            wz[d].wait_recv()
-        block = wt.at[pl.ds(pl.multiple_of(col_at(-d) * cs, 16), cs), half_lanes]
-        sib.append(send(block, block, sib_s.at[d - 1], sib_r.at[d - 1], sibling))
+        pass_on(0)
+        spread_rows(cut, 2 * cut)
+        for e in range(1, steps):
+            pass_on(e)
+            pass_again(e - 1)
+            if e > 1:
+                to_sibling(e - 2)
+        pass_again(steps - 1)
+        for e in range(max(steps - 2, 0), steps - 1):
+            to_sibling(e)
+        spread_rows(2 * cut, tile_rows)
+        halo_rows(x3, x_halo, x_copies, False)
+        to_sibling(steps - 1)
+    else:
+        spread_rows(cut, tile_rows)
+        for e in range(steps):
+            to_sibling(e)
+        halo_rows(x3, x_halo, x_copies, False)
     for copy in sib:
         copy.wait_recv()
 
@@ -272,9 +315,6 @@
         act(2 * t, conv_even)
         convolve(jnp.minimum(2 * t + 2, 3), conv_even)
         act(2 * t + 1, conv_odd)
-
-    feat_copy = pltpu.make_async_copy(feat_own, feat_ref, out_sem.at[0])
-    feat_copy.start()
 
     centre = pl.ds(chan, chan)
     g_copies = halo_copies(g3.at[1, :, centre], g3.at[tile_rows, :, centre], g_halo, 2)
@@ -337,6 +377,17 @@
         if not split:
             return []
         own = gathered.at[k, core, quad]
+        if k == 2:
+            return [
+                send(
+                    own,
+                    own,
+                    all_s.at[d - 1],
+                    all_r.at[my_row],
+                    ((my_row + d) % rows, my_col),
+                )
+                for d in range(1, rows)
+            ]
         return [
             send(
                 own, own, ag_s.at[k, d], ag_r.at[k, d], (((quad + d) % quads) * 2 + core, my_col)
@@ -345,6 +396,12 @@
         ]
 
     def after_quads(k, copies):
+        if split and k == 2:
+            for d in range(1, rows):
+                row = (my_row + d) % rows
+                got = gathered.at[k, row % 2, row // 2]
+                pltpu.make_async_copy(got, got, all_r.at[row]).wait()
+            return None
         for copy in copies:
             copy.wait_recv()
         own = gathered.at[k, core]
@@ -353,17 +410,13 @@
     scale = 1.0 / math.sqrt(tile_rows * width * rows * cols)
 
     def finish(k, copy):
-        copy.wait_recv()
+        if copy is not None:
+            copy.wait_recv()
         for h in range(2):
             value = gathered[k, h].astype(jnp.float32).reshape(cs, half_k) * scale
             for lane in range(0, half_k, 128):
                 tap, at = divmod(h * half_k + lane, chan)
                 wg_own[3 * k + tap, :, at : at + 128] = value[:, lane : lane + 128]
-        done = pltpu.make_async_copy(
-            wg_own.at[3 * k : 3 * k + 3], wg_ref.at[3 * k : 3 * k + 3], out_sem.at[2 + k]
-        )
-        done.start()
-        return done
 
     def input_part(b):
         acc = None
@@ -388,29 +441,33 @@
     flight[0] = after_siblings(0, flight[0])
     flight[2] = weight_part(2)
     flight[1] = after_siblings(1, flight[1])
+    flight[0] = after_phase(0, 0, flight[0])
+    flight[2] = after_siblings(2, flight[2])
     input_part(1)
-    flight[2] = after_siblings(2, flight[2])
-    for j in range(phases):
-        for k in range(3):
-            flight[k] = after_phase(k, j, flight[k])
-        if j == 0:
-            input_part(2)
+    flight[1] = after_phase(1, 0, flight[1])
+    for j in range(1, phases):
+        flight[0] = after_phase(0, j, flight[0])
+    flight[2] = after_phase(2, 0, flight[2])
+    input_part(2)
+    for j in range(1, phases):
+        flight[1] = after_phase(1, j, flight[1])
+    flight[0] = after_cols(0, flight[0])
+    for j in range(1, phases):
+        flight[2] = after_phase(2, j, flight[2])
     halo_rows(g3, g_halo, g_copies, True)
     input_part(0)
-    for k in range(3):
-        flight[k] = after_cols(k, flight[k])
+    flight[1] = after_cols(1, flight[1])
+    flight[0] = after_quads(0, flight[0])
+    flight[2] = after_cols(2, flight[2])
     input_part(3)
-    igrad_copy = pltpu.make_async_copy(igrad_own, igrad_ref, out_sem.at[1])
-    igrad_copy.start()
-    for k in range(3):
-        flight[k] = after_quads(k, flight[k])
-    for k in range(3):
-        flight[k] = finish(k, flight[k])
-
-    for copy in started:
+    flight[1] = after_quads(1, flight[1])
+    finish(0, flight[0])
+    finish(1, flight[1])
+    flight[2] = after_quads(2, flight[2])
+    finish(2, flight[2])
+
+    for copy in started + wz:
         copy.wait_send()
-    for copy in [feat_copy, igrad_copy] + flight:
-        copy.wait()
     for up, down in (x_copies, g_copies):
 
         @pl.when(has_up)
@@ -459,9 +516,6 @@
         vmem((tile_rows // 4, width + 16, out_chan), jnp.float32),
         vmem((tile_rows, width, chan), bf16),
         vmem((tile_rows, width, out_chan), bf16),
-        vmem((tile_rows, width, out_chan), bf16),
-        vmem((tile_rows, width, chan), bf16),
-        vmem((9, cs, chan), jnp.float32),
         vmem((2, width, chan), bf16),
         vmem((2, width, out_chan), bf16),
         vmem((3, 2, pieces, cols, rs, half), bf16),
@@ -471,18 +525,20 @@
     ]
     scratch += [vmem((3, n, cols, rs, half), bf16) for n in counts]
     scratch += [vmem((3, n, cols, rs, half), bf16) for n in counts[1:]]
-    scratch += [dma((11,)), dma((5,))]
+    scratch += [dma((11,))]
     for shape in (
         (4,),
-        (cols - 1,),
+        (cols,),
         (cols - 1, 3),
         (cols - 1,),
         (3, phases + 1),
         (3, cols - 1),
         (3, quads),
+        (rows,),
     ):
         scratch += [dma(shape), dma(shape)]
-    anywhere = pl.BlockSpec(memory_space=pl.ANY)
+    in_hbm = pl.BlockSpec(memory_space=pltpu.HBM)
+    in_vmem = pl.BlockSpec(memory_space=pltpu.VMEM)
     flops = 3 * 2 * tile_rows * width * 3 * taps * out_chan
     shapes = (
         jax.ShapeDtypeStruct((tile_rows, width, out_chan), bf16),
@@ -492,14 +548,14 @@
     results = pl.pallas_call(
         functools.partial(kernel, (rows, cols, quads, split, cs, rs)),
         out_shape=shapes,
-        in_specs=[anywhere, anywhere, pl.BlockSpec(memory_space=pltpu.VMEM), anywhere],
-        out_specs=(anywhere,) * 3,
+        in_specs=[in_hbm, in_hbm, in_vmem, in_hbm],
+        out_specs=(in_vmem,) * 3,
         scratch_shapes=scratch,
         cost_estimate=pl.CostEstimate(
             flops=flops, bytes_accessed=4 << 20, transcendentals=2 * tile_rows * width * out_chan
         ),
         compiler_params=pltpu.CompilerParams(
-            collective_id=0, has_side_effects=True, vmem_limit_bytes=60 << 20
+            collective_id=0, has_side_effects=True, vmem_limit_bytes=48 << 20
         ),
     )(
         images.reshape(tile_rows, width, chan),
@@ -510,10 +566,9 @@
     features, input_grad, wide_grad = pl.pallas_call(
         move,
         out_shape=shapes,
-        in_specs=[anywhere] * 3,
-        out_specs=(anywhere,) * 3,
+        in_specs=[in_vmem] * 3,
+        out_specs=(in_hbm,) * 3,
         scratch_shapes=[dma((3,))],
-        compiler_params=pltpu.CompilerParams(vmem_limit_bytes=60 << 20),
     )(*results)
     weight_grad = jnp.swapaxes(wide_grad.reshape(3, 3, cs, chan), 2, 3)
     return (features[None], input_grad[None], weight_grad)

time: 94.9 us -> 52.6 us (0.55)
  Pallas kernels: 93.5 us -> 45.5 us
  local copies, waits for them, and re-layouts: 0 us -> 6.14 us
    pallas_call x1, Pallas kernels: 50.8 us -> 2.56 us  [on_device(): pl.pallas_call(move, out_shape=shapes, in_specs=[in_vmem] * 3, out_specs=...]
    unnamed x0 -> x14, local copies, waits for them, and re-layouts: none -> 6.14 us
where the time goes in v3:
time: 52.6 us; the launch traced here: 52.3 us
  Pallas kernels  45.5 us (87%)
  local copies, waits for them, and re-layouts  6.14 us (12%)
  between operations  0.66 us (1%)
    pallas_call x1, Pallas kernels, on_device(): pl.pallas_call(functools.partial(kernel, (rows, cols, quads, split, cs, r...  43 us
    unnamed x14, local copies, waits for them, and re-layouts  6.14 us
    pallas_call x1, Pallas kernels, on_device(): pl.pallas_call(move, out_shape=shapes, in_specs=[in_vmem] * 3, out_specs=...  2.56 us

profile of v3, /device:TPU:0, one launch (start us, length us, event | category | flops | bytes accessed | tf_op | source)
XLA Modules:
  0.0 52.3 jit_solution(663684066694907704)
XLA Ops:
  0.6 0.0 copy-start.6
  0.6 0.7 %copy-done.6 = f32[256]{0:T(256)S(1)} copy-done((f32[256]{0:T(256)S(1)}, f32[256]{0:T(256)}, u32[]{:S(2)}) %copy-start.6) | copy-done | bytes 1048
  1.3 0.0 copy-start.3
  1.3 1.0 %copy-done.3 = bf16[1,8,128,256]{3,2,1,0:T(8,128)(2,1)S(1)} copy-done((bf16[1,8,128,256]{3,2,1,0:T(8,128)(2,1)S(1)}, bf16[1,8,128,256]{3,2,1,0:T(8,128)(2,1)}, u32[]{:S(2)}) %copy-start.3) | copy-done | bytes 524312
  2.4 0.0 copy-start.4
  2.4 1.0 %copy-done.4 = bf16[1,8,128,256]{3,2,1,0:T(8,128)(2,1)S(1)} copy-done((bf16[1,8,128,256]{3,2,1,0:T(8,128)(2,1)S(1)}, bf16[1,8,128,256]{3,2,1,0:T(8,128)(2,1)}, u32[]{:S(2)}) %copy-start.4) | copy-done | bytes 524312
  3.4 0.0 copy-start.5
  3.4 1.0 %copy-done.5 = bf16[3,3,256,64]{2,3,1,0:T(8,128)(2,1)S(1)} copy-done((bf16[3,3,256,64]{2,3,1,0:T(8,128)(2,1)S(1)}, bf16[3,3,256,64]{2,3,1,0:T(8,128)(2,1)}, u32[]{:S(2)}) %copy-start.5) | copy-done | bytes 294936
  4.4 43.0 %shard_map.67 = (bf16[8,128,256]{2,1,0:T(8,128)(2,1)S(1)}, bf16[8,128,256]{2,1,0:T(8,128)(2,1)S(1)}, f32[9,64,256]{2,1,0:T(8,128)S(1)}) custom-call(bf16[8,128,256]{2,1,0:T(8,128)(2,1)S(1)} %bitcast.11, bf16[9,64,256]{2,1,0:T(8,128)(2,1)S(1)} %bitcast.13, f32[1,256]{1,0:T(1,128)S(1)} %bitcast.14, bf16[8,128,256]{2,1,0:T(8,128)(2,1)S(1)} %bitcast.12), custom_call_target="tpu_custom_call" | custom-call | flops 3623878656 | bytes 4194304 | tf_op jit(solution)/shard_map/pallas_call | solution.py:548
  47.3 0.0 copy-start
  47.4 0.8 %copy-done = f32[9,64,256]{2,1,0:T(8,128)} copy-done((f32[9,64,256]{2,1,0:T(8,128)}, f32[9,64,256]{2,1,0:T(8,128)S(1)}, u32[]{:S(2)}) %copy-start) | copy-done | bytes 589848
  48.2 0.0 copy-start.1
  48.2 0.8 %copy-done.1 = bf16[8,128,256]{2,1,0:T(8,128)(2,1)} copy-done((bf16[8,128,256]{2,1,0:T(8,128)(2,1)}, bf16[8,128,256]{2,1,0:T(8,128)(2,1)S(1)}, u32[]{:S(2)}) %copy-start.1) | copy-done | bytes 524312
  49.0 0.0 copy-start.2
  49.0 0.8 %copy-done.2 = bf16[8,128,256]{2,1,0:T(8,128)(2,1)} copy-done((bf16[8,128,256]{2,1,0:T(8,128)(2,1)}, bf16[8,128,256]{2,1,0:T(8,128)(2,1)S(1)}, u32[]{:S(2)}) %copy-start.2) | copy-done | bytes 524312
  49.8 2.6 %shard_map.68 = (bf16[8,128,256]{2,1,0:T(8,128)(2,1)}, bf16[8,128,256]{2,1,0:T(8,128)(2,1)}, f32[9,64,256]{2,1,0:T(8,128)}) custom-call(bf16[8,128,256]{2,1,0:T(8,128)(2,1)} %copy-done.1, bf16[8,128,256]{2,1,0:T(8,128)(2,1)} %copy-done.2, f32[9,64,256]{2,1,0:T(8,128)} %copy-done), custom_call_target="tpu_custom_call" | custom-call | tf_op jit(solution)/shard_map/pallas_call | solution.py:566
Async XLA Ops:
  0.6 0.7 %copy-start.6 = (f32[256]{0:T(256)S(1)}, f32[256]{0:T(256)}, u32[]{:S(2)}) copy-start(f32[256]{0:T(256)} %param.6) | copy-start | bytes 3076
  1.3 1.0 %copy-start.3 = (bf16[1,8,128,256]{3,2,1,0:T(8,128)(2,1)S(1)}, bf16[1,8,128,256]{3,2,1,0:T(8,128)(2,1)}, u32[]{:S(2)}) copy-start(bf16[1,8,128,256]{3,2,1,0:T(8,128)(2,1)} %param.4) | copy-start | bytes 1572868
  2.4 1.0 %copy-start.4 = (bf16[1,8,128,256]{3,2,1,0:T(8,128)(2,1)S(1)}, bf16[1,8,128,256]{3,2,1,0:T(8,128)(2,1)}, u32[]{:S(2)}) copy-start(bf16[1,8,128,256]{3,2,1,0:T(8,128)(2,1)} %param.7) | copy-start | bytes 1572868
  3.4 1.0 %copy-start.5 = (bf16[3,3,256,64]{2,3,1,0:T(8,128)(2,1)S(1)}, bf16[3,3,256,64]{2,3,1,0:T(8,128)(2,1)}, u32[]{:S(2)}) copy-start(bf16[3,3,256,64]{2,3,1,0:T(8,128)(2,1)} %param.5) | copy-start | bytes 884740
  47.3 0.8 %copy-start = (f32[9,64,256]{2,1,0:T(8,128)}, f32[9,64,256]{2,1,0:T(8,128)S(1)}, u32[]{:S(2)}) copy-start(f32[9,64,256]{2,1,0:T(8,128)S(1)} %get-tuple-element.11.refs_2_) | copy-start | bytes 1769476
  48.2 0.8 %copy-start.1 = (bf16[8,128,256]{2,1,0:T(8,128)(2,1)}, bf16[8,128,256]{2,1,0:T(8,128)(2,1)S(1)}, u32[]{:S(2)}) copy-start(bf16[8,128,256]{2,1,0:T(8,128)(2,1)S(1)} %get-tuple-element.9.refs_0_) | copy-start | bytes 1572868
  49.0 0.8 %copy-start.2 = (bf16[8,128,256]{2,1,0:T(8,128)(2,1)}, bf16[8,128,256]{2,1,0:T(8,128)(2,1)S(1)}, u32[]{:S(2)}) copy-start(bf16[8,128,256]{2,1,0:T(8,128)(2,1)S(1)} %get-tuple-element.10.refs_1_) | copy-start | bytes 1572868

commit v4 on v3

--- a/solution.py
+++ b/solution.py
@@ -37,18 +37,20 @@
     w_ref,
     gain_ref,
     cot_ref,
-    feat_own,
-    igrad_own,
-    wg_own,
+    feat_ref,
+    igrad_ref,
+    wg_ref,
     wt,
     x3,
     g3,
     gt,
-    conv_even,
-    conv_odd,
+    conv,
     g_pad,
     x_own,
     cot_own,
+    feat_own,
+    igrad_own,
+    wg_own,
     x_halo,
     g_halo,
     parts,
@@ -60,7 +62,7 @@
     rows, cols, quads, split, cs, rs = plan
     phases = quads.bit_length() - 1
     totals, totals_in = rest[: phases + 1], rest[phases + 1 : 2 * phases + 1]
-    (in_sem, halo_s, halo_r, wz_s, wz_r, wq_s, wq_r, sib_s, sib_r, ph_s, ph_r, z_s, z_r, ag_s, ag_r, all_s, all_r) = rest[
+    (in_sem, out_sem, halo_s, halo_r, wz_s, wz_r, wq_s, wq_r, sib_s, sib_r, ph_s, ph_r, z_s, z_r, ag_s, ag_r, all_s, all_r) = rest[
         2 * phases + 1 :
     ]
     tile_rows, width, chan = x_ref.shape
@@ -276,53 +278,59 @@
         copy.wait_recv()
 
     gain = gain_ref[...]
-    quarter = tile_rows // 4
+    part_rows = tile_rows // 2
     strip = 32
 
-    def convolve(b, into):
+    @pl.loop(0, 2)
+    def _(b):
         acc = None
         for a in range(3):
             term = lax.dot_general(
-                x3[pl.ds(b * quarter + a, quarter)].reshape(quarter * width, taps),
+                x3[pl.ds(b * part_rows + a, part_rows)].reshape(part_rows * width, taps),
                 wt[:, a * taps : (a + 1) * taps],
                 NT,
                 preferred_element_type=jnp.float32,
             )
             acc = term if acc is None else acc + term
-        into[...] = acc.reshape(quarter, width, out_chan)
-
-    def act(b, source):
-        for r in range(quarter):
-            i = b * quarter + r
-            for first in range(0, width, strip):
-                span = slice(first, first + strip)
-                outputs, grad_pre = norm_act(source[r, span], cot_own[i, span], gain)
-                feat_own[i, span] = outputs
-                g_pad[r, 8 + first : 8 + first + strip] = grad_pre
-            value = g_pad[r, 8 : 8 + width].astype(jnp.bfloat16)
-            g3[i + 1, :, 0:out_chan] = g_pad[r, 9 : 9 + width].astype(jnp.bfloat16)
-            g3[i + 1, :, out_chan : 2 * out_chan] = value
-            g3[i + 1, :, 2 * out_chan :] = g_pad[r, 7 : 7 + width].astype(jnp.bfloat16)
-            gt[:, pl.ds(pl.multiple_of(i * width, 128), width)] = value.T
+        conv[pl.ds(b * part_rows, part_rows)] = acc.reshape(part_rows, width, out_chan)
 
     g_pad[...] = jnp.zeros(g_pad.shape, g_pad.dtype)
     cot_copy.wait()
-    convolve(0, conv_even)
-
-    @pl.loop(0, 2)
-    def _(t):
-        convolve(2 * t + 1, conv_odd)
-        act(2 * t, conv_even)
-        convolve(jnp.minimum(2 * t + 2, 3), conv_even)
-        act(2 * t + 1, conv_odd)
+
+    @pl.loop(0, tile_rows)
+    def _(i):
+        for first in range(0, width, strip):
+            span = slice(first, first + strip)
+            outputs, grad_pre = norm_act(conv[i, span], cot_own[i, span], gain)
+            feat_own[i, span] = outputs
+            g_pad[8 + first : 8 + first + strip] = grad_pre
+        value = g_pad[8 : 8 + width].astype(jnp.bfloat16)
+        g3[i + 1, :, 0:out_chan] = g_pad[9 : 9 + width].astype(jnp.bfloat16)
+        g3[i + 1, :, out_chan : 2 * out_chan] = value
+        g3[i + 1, :, 2 * out_chan :] = g_pad[7 : 7 + width].astype(jnp.bfloat16)
+        gt[:, pl.ds(pl.multiple_of(i * width, 128), width)] = value.T
+
+    feat_copy = pltpu.make_async_copy(feat_own, feat_ref, out_sem.at[0])
+    feat_copy.start()
 
     centre = pl.ds(chan, chan)
     g_copies = halo_copies(g3.at[1, :, centre], g3.at[tile_rows, :, centre], g_halo, 2)
 
-    def weight_part(k):
+    def to_pair(k):
+        return pltpu.make_async_remote_copy(
+            src_ref=parts.at[k, 1 - core],
+            dst_ref=parts_in.at[k],
+            send_sem=ph_s.at[k, phases],
+            recv_sem=ph_r.at[k, phases],
+            device_id=sibling,
+            device_id_type=MESH,
+        )
+
+    @pl.loop(0, 3)
+    def _(k):
         acc = jnp.dot(
             gt[...],
-            x3[k : k + tile_rows].reshape(tile_rows * width, taps),
+            x3[pl.ds(k, tile_rows)].reshape(tile_rows * width, taps),
             preferred_element_type=jnp.float32,
         ).astype(jnp.bfloat16)
         for h in range(2):
@@ -331,9 +339,7 @@
                 for c in range(cols):
                     first = c * cs + s * rs
                     parts[k, h, at, c] = acc[first : first + rs, h * half_k : (h + 1) * half_k]
-        return send(
-            parts.at[k, 1 - core], parts_in.at[k], ph_s.at[k, phases], ph_r.at[k, phases], sibling
-        )
+        to_pair(k).start()
 
     def add(one, two):
         return (one.astype(jnp.float32) + two.astype(jnp.float32)).astype(jnp.bfloat16)
@@ -417,57 +423,61 @@
             for lane in range(0, half_k, 128):
                 tap, at = divmod(h * half_k + lane, chan)
                 wg_own[3 * k + tap, :, at : at + 128] = value[:, lane : lane + 128]
+        done = pltpu.make_async_copy(
+            wg_own.at[3 * k : 3 * k + 3], wg_ref.at[3 * k : 3 * k + 3], out_sem.at[2 + k]
+        )
+        done.start()
+        return done
 
     def input_part(b):
         acc = None
         for a in range(3):
             for c in range(3):
-                first = b * quarter + 2 - a
+                first = b * part_rows + 2 - a
                 term = jnp.dot(
-                    g3[first : first + quarter, :, c * chan : (c + 1) * chan].reshape(
-                        quarter * width, out_chan
+                    g3[first : first + part_rows, :, c * chan : (c + 1) * chan].reshape(
+                        part_rows * width, out_chan
                     ),
                     wt[:, a * taps + c * chan : a * taps + (c + 1) * chan],
                     preferred_element_type=jnp.float32,
                 )
                 acc = term if acc is None else acc + term
-        igrad_own[b * quarter : (b + 1) * quarter] = acc.astype(jnp.bfloat16).reshape(
-            quarter, width, chan
-        )
-
-    flight = [None] * 3
-    flight[0] = weight_part(0)
-    flight[1] = weight_part(1)
-    flight[0] = after_siblings(0, flight[0])
-    flight[2] = weight_part(2)
-    flight[1] = after_siblings(1, flight[1])
+        igrad_own[b * part_rows : (b + 1) * part_rows] = acc.astype(jnp.bfloat16).reshape(
+            part_rows, width, chan
+        )
+
+    flight = [to_pair(k) for k in range(3)]
+    started.extend(flight)
+    for k in range(3):
+        flight[k] = after_siblings(k, flight[k])
+    halo_rows(g3, g_halo, g_copies, True)
     flight[0] = after_phase(0, 0, flight[0])
-    flight[2] = after_siblings(2, flight[2])
-    input_part(1)
     flight[1] = after_phase(1, 0, flight[1])
+    input_part(0)
     for j in range(1, phases):
         flight[0] = after_phase(0, j, flight[0])
     flight[2] = after_phase(2, 0, flight[2])
-    input_part(2)
     for j in range(1, phases):
         flight[1] = after_phase(1, j, flight[1])
     flight[0] = after_cols(0, flight[0])
     for j in range(1, phases):
         flight[2] = after_phase(2, j, flight[2])
-    halo_rows(g3, g_halo, g_copies, True)
-    input_part(0)
     flight[1] = after_cols(1, flight[1])
+    input_part(1)
+    igrad_copy = pltpu.make_async_copy(igrad_own, igrad_ref, out_sem.at[1])
+    igrad_copy.start()
     flight[0] = after_quads(0, flight[0])
     flight[2] = after_cols(2, flight[2])
-    input_part(3)
     flight[1] = after_quads(1, flight[1])
-    finish(0, flight[0])
-    finish(1, flight[1])
+    flight[0] = finish(0, flight[0])
+    flight[1] = finish(1, flight[1])
     flight[2] = after_quads(2, flight[2])
-    finish(2, flight[2])
+    flight[2] = finish(2, flight[2])
 
     for copy in started + wz:
         copy.wait_send()
+    for copy in [feat_copy, igrad_copy] + flight:
+        copy.wait()
     for up, down in (x_copies, g_copies):
 
         @pl.when(has_up)
@@ -477,17 +487,6 @@
         @pl.when(has_down)
         def _():
             down.wait_send()
-
-
-def move(*refs):
-    count = len(refs) // 2
-    copies = [
-        pltpu.make_async_copy(refs[i], refs[count + i], refs[-1].at[i]) for i in range(count)
-    ]
-    for copy in copies:
-        copy.start()
-    for copy in copies:
-        copy.wait()
 
 
 def on_device(images, weight, norm_gain, cotangent):
@@ -511,11 +510,13 @@
         vmem((tile_rows + 2, width, taps), bf16),
         vmem((tile_rows + 2, width, 3 * out_chan), bf16),
         vmem((out_chan, tile_rows * width), bf16),
-        vmem((tile_rows // 4, width, out_chan), jnp.float32),
-        vmem((tile_rows // 4, width, out_chan), jnp.float32),
-        vmem((tile_rows // 4, width + 16, out_chan), jnp.float32),
+        vmem((tile_rows, width, out_chan), jnp.float32),
+        vmem((width + 16, out_chan), jnp.float32),
         vmem((tile_rows, width, chan), bf16),
         vmem((tile_rows, width, out_chan), bf16),
+        vmem((tile_rows, width, out_chan), bf16),
+        vmem((tile_rows, width, chan), bf16),
+        vmem((9, cs, chan), jnp.float32),
         vmem((2, width, chan), bf16),
         vmem((2, width, out_chan), bf16),
         vmem((3, 2, pieces, cols, rs, half), bf16),
@@ -525,7 +526,7 @@
     ]
     scratch += [vmem((3, n, cols, rs, half), bf16) for n in counts]
     scratch += [vmem((3, n, cols, rs, half), bf16) for n in counts[1:]]
-    scratch += [dma((11,))]
+    scratch += [dma((11,)), dma((5,))]
     for shape in (
         (4,),
         (cols,),
@@ -545,17 +546,17 @@
         jax.ShapeDtypeStruct((tile_rows, width, chan), bf16),
         jax.ShapeDtypeStruct((9, cs, chan), jnp.float32),
     )
-    results = pl.pallas_call(
+    features, input_grad, wide_grad = pl.pallas_call(
         functools.partial(kernel, (rows, cols, quads, split, cs, rs)),
         out_shape=shapes,
         in_specs=[in_hbm, in_hbm, in_vmem, in_hbm],
-        out_specs=(in_vmem,) * 3,
+        out_specs=(in_hbm,) * 3,
         scratch_shapes=scratch,
         cost_estimate=pl.CostEstimate(
             flops=flops, bytes_accessed=4 << 20, transcendentals=2 * tile_rows * width * out_chan
         ),
         compiler_params=pltpu.CompilerParams(
-            collective_id=0, has_side_effects=True, vmem_limit_bytes=48 << 20
+            collective_id=0, has_side_effects=True, vmem_limit_bytes=60 << 20
         ),
     )(
         images.reshape(tile_rows, width, chan),
@@ -563,13 +564,6 @@
         norm_gain.reshape(1, out_chan),
         cotangent.reshape(tile_rows, width, out_chan),
     )
-    features, input_grad, wide_grad = pl.pallas_call(
-        move,
-        out_shape=shapes,
-        in_specs=[in_vmem] * 3,
-        out_specs=(in_hbm,) * 3,
-        scratch_shapes=[dma((3,))],
-    )(*results)
     weight_grad = jnp.swapaxes(wide_grad.reshape(3, 3, cs, chan), 2, 3)
     return (features[None], input_grad[None], weight_grad)
 

time: 52.6 us -> 51.2 us (0.973)
  local copies, waits for them, and re-layouts: 6.14 us -> 4 us
  Pallas kernels: 45.5 us -> 46.4 us
    pallas_call x1, Pallas kernels: 43 us -> 46.4 us  [on_device(): pl.pallas_call(functools.partial(kernel, (rows, cols, quads, split, cs, r...]
    pallas_call x1 -> x0, Pallas kernels: 2.56 us -> none  [on_device(): pl.pallas_call(move, out_shape=shapes, in_specs=[in_vmem] * 3, out_specs=...]
    unnamed x14 -> x7, local copies, waits for them, and re-layouts: 6.14 us -> 4 us
where the time goes in v4:
time: 51.2 us; the launch traced here: 51 us
  Pallas kernels  46.4 us (91%)
  local copies, waits for them, and re-layouts  4 us (8%)
  between operations  0.65 us (1%)
    pallas_call x1, Pallas kernels, on_device(): pl.pallas_call(functools.partial(kernel, (rows, cols, quads, split, cs, r...  46.4 us
    unnamed x7, local copies, waits for them, and re-layouts  4 us

profile of v4, /device:TPU:0, one launch (start us, length us, event | category | flops | bytes accessed | tf_op | source)
XLA Modules:
  0.0 51.0 jit_solution(4307993394111704689)
XLA Ops:
  0.6 46.4 %shard_map.67 = (bf16[8,128,256]{2,1,0:T(8,128)(2,1)}, bf16[8,128,256]{2,1,0:T(8,128)(2,1)}, f32[9,64,256]{2,1,0:T(8,128)}) custom-call(bf16[8,128,256]{2,1,0:T(8,128)(2,1)} %bitcast.14, bf16[9,64,256]{2,1,0:T(8,128)(2,1)} %bitcast.16, f32[1,256]{1,0:T(1,128)} %bitcast.17, bf16[8,128,256]{2,1,0:T(8,128)(2,1)} %bitcast.15), custom_call_target="tpu_custom_call" | custom-call | flops 3623878656 | bytes 4194304 | tf_op jit(solution)/shard_map/pallas_call | solution.py:549
  47.0 0.0 copy-start.1
  47.0 1.9 %copy.10 = bf16[1,8,128,256]{3,2,1,0:T(8,128)(2,1)} copy(bf16[1,8,128,256]{3,2,1,0:T(8,128)(2,1)} %bitcast.13) | data formatting | bytes 1048576
  48.9 0.0 copy-done.1
  48.9 0.0 copy-start
  48.9 0.8 %copy.11 = bf16[1,8,128,256]{3,2,1,0:T(8,128)(2,1)} copy(bf16[1,8,128,256]{3,2,1,0:T(8,128)(2,1)S(1)} %bitcast.12) | data formatting | bytes 1048576
  49.7 0.5 copy-done
  50.2 0.8 %copy.12 = f32[3,3,256,64]{2,3,1,0:T(8,128)} copy(f32[3,3,256,64]{2,3,1,0:T(8,128)S(1)} %bitcast.11) | data formatting | bytes 1179648
Async XLA Ops:
  47.0 1.9 %copy-start.1 = (bf16[8,128,256]{2,1,0:T(8,128)(2,1)S(1)}, bf16[8,128,256]{2,1,0:T(8,128)(2,1)}, u32[]{:S(2)}) copy-start(bf16[8,128,256]{2,1,0:T(8,128)(2,1)} %get-tuple-element.7) | copy-start | bytes 1572868
  48.9 1.3 %copy-start = (f32[9,64,256]{2,1,0:T(8,128)S(1)}, f32[9,64,256]{2,1,0:T(8,128)}, u32[]{:S(2)}) copy-start(f32[9,64,256]{2,1,0:T(8,128)} %get-tuple-element.8) | copy-start | bytes 1769476

commit v5 on v3

--- a/solution.py
+++ b/solution.py
@@ -37,9 +37,9 @@
     w_ref,
     gain_ref,
     cot_ref,
-    feat_own,
-    igrad_own,
-    wg_own,
+    feat_ref,
+    igrad_ref,
+    wg_ref,
     wt,
     x3,
     g3,
@@ -49,6 +49,9 @@
     g_pad,
     x_own,
     cot_own,
+    feat_own,
+    igrad_own,
+    wg_own,
     x_halo,
     g_halo,
     parts,
@@ -60,7 +63,7 @@
     rows, cols, quads, split, cs, rs = plan
     phases = quads.bit_length() - 1
     totals, totals_in = rest[: phases + 1], rest[phases + 1 : 2 * phases + 1]
-    (in_sem, halo_s, halo_r, wz_s, wz_r, wq_s, wq_r, sib_s, sib_r, ph_s, ph_r, z_s, z_r, ag_s, ag_r, all_s, all_r) = rest[
+    (in_sem, out_sem, halo_s, halo_r, wz_s, wz_r, wq_s, wq_r, sib_s, sib_r, ph_s, ph_r, z_s, z_r, ag_s, ag_r, all_s, all_r) = rest[
         2 * phases + 1 :
     ]
     tile_rows, width, chan = x_ref.shape
@@ -315,6 +318,9 @@
         act(2 * t, conv_even)
         convolve(jnp.minimum(2 * t + 2, 3), conv_even)
         act(2 * t + 1, conv_odd)
+
+    feat_copy = pltpu.make_async_copy(feat_own, feat_ref, out_sem.at[0])
+    feat_copy.start()
 
     centre = pl.ds(chan, chan)
     g_copies = halo_copies(g3.at[1, :, centre], g3.at[tile_rows, :, centre], g_halo, 2)
@@ -417,6 +423,11 @@
             for lane in range(0, half_k, 128):
                 tap, at = divmod(h * half_k + lane, chan)
                 wg_own[3 * k + tap, :, at : at + 128] = value[:, lane : lane + 128]
+        done = pltpu.make_async_copy(
+            wg_own.at[3 * k : 3 * k + 3], wg_ref.at[3 * k : 3 * k + 3], out_sem.at[2 + k]
+        )
+        done.start()
+        return done
 
     def input_part(b):
         acc = None
@@ -460,14 +471,18 @@
     flight[0] = after_quads(0, flight[0])
     flight[2] = after_cols(2, flight[2])
     input_part(3)
+    igrad_copy = pltpu.make_async_copy(igrad_own, igrad_ref, out_sem.at[1])
+    igrad_copy.start()
     flight[1] = after_quads(1, flight[1])
-    finish(0, flight[0])
-    finish(1, flight[1])
+    flight[0] = finish(0, flight[0])
+    flight[1] = finish(1, flight[1])
     flight[2] = after_quads(2, flight[2])
-    finish(2, flight[2])
+    flight[2] = finish(2, flight[2])
 
     for copy in started + wz:
         copy.wait_send()
+    for copy in [feat_copy, igrad_copy] + flight:
+        copy.wait()
     for up, down in (x_copies, g_copies):
 
         @pl.when(has_up)
@@ -477,17 +492,6 @@
         @pl.when(has_down)
         def _():
             down.wait_send()
-
-
-def move(*refs):
-    count = len(refs) // 2
-    copies = [
-        pltpu.make_async_copy(refs[i], refs[count + i], refs[-1].at[i]) for i in range(count)
-    ]
-    for copy in copies:
-        copy.start()
-    for copy in copies:
-        copy.wait()
 
 
 def on_device(images, weight, norm_gain, cotangent):
@@ -516,6 +520,9 @@
         vmem((tile_rows // 4, width + 16, out_chan), jnp.float32),
         vmem((tile_rows, width, chan), bf16),
         vmem((tile_rows, width, out_chan), bf16),
+        vmem((tile_rows, width, out_chan), bf16),
+        vmem((tile_rows, width, chan), bf16),
+        vmem((9, cs, chan), jnp.float32),
         vmem((2, width, chan), bf16),
         vmem((2, width, out_chan), bf16),
         vmem((3, 2, pieces, cols, rs, half), bf16),
@@ -525,7 +532,7 @@
     ]
     scratch += [vmem((3, n, cols, rs, half), bf16) for n in counts]
     scratch += [vmem((3, n, cols, rs, half), bf16) for n in counts[1:]]
-    scratch += [dma((11,))]
+    scratch += [dma((11,)), dma((5,))]
     for shape in (
         (4,),
         (cols,),
@@ -545,17 +552,17 @@
         jax.ShapeDtypeStruct((tile_rows, width, chan), bf16),
         jax.ShapeDtypeStruct((9, cs, chan), jnp.float32),
     )
-    results = pl.pallas_call(
+    features, input_grad, wide_grad = pl.pallas_call(
         functools.partial(kernel, (rows, cols, quads, split, cs, rs)),
         out_shape=shapes,
         in_specs=[in_hbm, in_hbm, in_vmem, in_hbm],
-        out_specs=(in_vmem,) * 3,
+        out_specs=(in_hbm,) * 3,
         scratch_shapes=scratch,
         cost_estimate=pl.CostEstimate(
             flops=flops, bytes_accessed=4 << 20, transcendentals=2 * tile_rows * width * out_chan
         ),
         compiler_params=pltpu.CompilerParams(
-            collective_id=0, has_side_effects=True, vmem_limit_bytes=48 << 20
+            collective_id=0, has_side_effects=True, vmem_limit_bytes=60 << 20
         ),
     )(
         images.reshape(tile_rows, width, chan),
@@ -563,13 +570,6 @@
         norm_gain.reshape(1, out_chan),
         cotangent.reshape(tile_rows, width, out_chan),
     )
-    features, input_grad, wide_grad = pl.pallas_call(
-        move,
-        out_shape=shapes,
-        in_specs=[in_vmem] * 3,
-        out_specs=(in_hbm,) * 3,
-        scratch_shapes=[dma((3,))],
-    )(*results)
     weight_grad = jnp.swapaxes(wide_grad.reshape(3, 3, cs, chan), 2, 3)
     return (features[None], input_grad[None], weight_grad)
 

time: 52.6 us -> 49.2 us (0.935)
  local copies, waits for them, and re-layouts: 6.14 us -> 4 us
  Pallas kernels: 45.5 us -> 44.3 us
    pallas_call x1 -> x0, Pallas kernels: 2.56 us -> none  [on_device(): pl.pallas_call(move, out_shape=shapes, in_specs=[in_vmem] * 3, out_specs=...]
    unnamed x14 -> x7, local copies, waits for them, and re-layouts: 6.14 us -> 4 us
    pallas_call x1, Pallas kernels: 43 us -> 44.3 us  [on_device(): pl.pallas_call(functools.partial(kernel, (rows, cols, quads, split, cs, r...]
where the time goes in v5:
time: 49.2 us; the launch traced here: 48.9 us
  Pallas kernels  44.3 us (90%)
  local copies, waits for them, and re-layouts  4 us (8%)
  between operations  0.65 us (1%)
    pallas_call x1, Pallas kernels, on_device(): pl.pallas_call(functools.partial(kernel, (rows, cols, quads, split, cs, r...  44.3 us
    unnamed x7, local copies, waits for them, and re-layouts  4 us

profile of v5, /device:TPU:0, one launch (start us, length us, event | category | flops | bytes accessed | tf_op | source)
XLA Modules:
  0.0 48.9 jit_solution(4124603984312172559)
XLA Ops:
  0.6 44.3 %shard_map.67 = (bf16[8,128,256]{2,1,0:T(8,128)(2,1)}, bf16[8,128,256]{2,1,0:T(8,128)(2,1)}, f32[9,64,256]{2,1,0:T(8,128)}) custom-call(bf16[8,128,256]{2,1,0:T(8,128)(2,1)} %bitcast.14, bf16[9,64,256]{2,1,0:T(8,128)(2,1)} %bitcast.16, f32[1,256]{1,0:T(1,128)} %bitcast.17, bf16[8,128,256]{2,1,0:T(8,128)(2,1)} %bitcast.15), custom_call_target="tpu_custom_call" | custom-call | flops 3623878656 | bytes 4194304 | tf_op jit(solution)/shard_map/pallas_call | solution.py:555
  44.9 0.0 copy-start.1
  44.9 1.9 %copy.10 = bf16[1,8,128,256]{3,2,1,0:T(8,128)(2,1)} copy(bf16[1,8,128,256]{3,2,1,0:T(8,128)(2,1)} %bitcast.13) | data formatting | bytes 1048576
  46.9 0.0 copy-done.1
  46.9 0.0 copy-start
  46.9 0.8 %copy.11 = bf16[1,8,128,256]{3,2,1,0:T(8,128)(2,1)} copy(bf16[1,8,128,256]{3,2,1,0:T(8,128)(2,1)S(1)} %bitcast.12) | data formatting | bytes 1048576
  47.7 0.5 copy-done
  48.1 0.8 %copy.12 = f32[3,3,256,64]{2,3,1,0:T(8,128)} copy(f32[3,3,256,64]{2,3,1,0:T(8,128)S(1)} %bitcast.11) | data formatting | bytes 1179648
Async XLA Ops:
  44.9 1.9 %copy-start.1 = (bf16[8,128,256]{2,1,0:T(8,128)(2,1)S(1)}, bf16[8,128,256]{2,1,0:T(8,128)(2,1)}, u32[]{:S(2)}) copy-start(bf16[8,128,256]{2,1,0:T(8,128)(2,1)} %get-tuple-element.7) | copy-start | bytes 1572868
  46.9 1.3 %copy-start = (f32[9,64,256]{2,1,0:T(8,128)S(1)}, f32[9,64,256]{2,1,0:T(8,128)}, u32[]{:S(2)}) copy-start(f32[9,64,256]{2,1,0:T(8,128)} %get-tuple-element.8) | copy-start | bytes 1769476

commit v6 on v5

--- a/solution.py
+++ b/solution.py
@@ -312,12 +312,11 @@
     cot_copy.wait()
     convolve(0, conv_even)
 
-    @pl.loop(0, 2)
-    def _(t):
-        convolve(2 * t + 1, conv_odd)
-        act(2 * t, conv_even)
-        convolve(jnp.minimum(2 * t + 2, 3), conv_even)
-        act(2 * t + 1, conv_odd)
+    buffers = (conv_even, conv_odd)
+    for b in range(4):
+        if b < 3:
+            convolve(b + 1, buffers[(b + 1) % 2])
+        act(b, buffers[b % 2])
 
     feat_copy = pltpu.make_async_copy(feat_own, feat_ref, out_sem.at[0])
     feat_copy.start()

time: 49.2 us -> 48.6 us (0.988)
  Pallas kernels: 44.3 us -> 43.7 us
    pallas_call x1, Pallas kernels: 44.3 us -> 43.7 us  [on_device(): pl.pallas_call(functools.partial(kernel, (rows, cols, quads, split, cs, r...]
where the time goes in v6:
time: 48.6 us; the launch traced here: 48.3 us
  Pallas kernels  43.7 us (90%)
  local copies, waits for them, and re-layouts  4 us (8%)
  between operations  0.65 us (1%)
    pallas_call x1, Pallas kernels, on_device(): pl.pallas_call(functools.partial(kernel, (rows, cols, quads, split, cs, r...  43.7 us
    unnamed x7, local copies, waits for them, and re-layouts  4 us

profile of v6, /device:TPU:0, one launch (start us, length us, event | category | flops | bytes accessed | tf_op | source)
XLA Modules:
  0.0 48.3 jit_solution(5396401106779930944)
XLA Ops:
  0.6 43.7 %shard_map.67 = (bf16[8,128,256]{2,1,0:T(8,128)(2,1)}, bf16[8,128,256]{2,1,0:T(8,128)(2,1)}, f32[9,64,256]{2,1,0:T(8,128)}) custom-call(bf16[8,128,256]{2,1,0:T(8,128)(2,1)} %bitcast.14, bf16[9,64,256]{2,1,0:T(8,128)(2,1)} %bitcast.16, f32[1,256]{1,0:T(1,128)} %bitcast.17, bf16[8,128,256]{2,1,0:T(8,128)(2,1)} %bitcast.15), custom_call_target="tpu_custom_call" | custom-call | flops 3623878656 | bytes 4194304 | tf_op jit(solution)/shard_map/pallas_call | solution.py:554
  44.3 0.0 copy-start.1
  44.3 1.9 %copy.10 = bf16[1,8,128,256]{3,2,1,0:T(8,128)(2,1)} copy(bf16[1,8,128,256]{3,2,1,0:T(8,128)(2,1)} %bitcast.13) | data formatting | bytes 1048576
  46.3 0.0 copy-done.1
  46.3 0.0 copy-start
  46.3 0.8 %copy.11 = bf16[1,8,128,256]{3,2,1,0:T(8,128)(2,1)} copy(bf16[1,8,128,256]{3,2,1,0:T(8,128)(2,1)S(1)} %bitcast.12) | data formatting | bytes 1048576
  47.1 0.5 copy-done
  47.5 0.8 %copy.12 = f32[3,3,256,64]{2,3,1,0:T(8,128)} copy(f32[3,3,256,64]{2,3,1,0:T(8,128)S(1)} %bitcast.11) | data formatting | bytes 1179648
Async XLA Ops:
  44.3 1.9 %copy-start.1 = (bf16[8,128,256]{2,1,0:T(8,128)(2,1)S(1)}, bf16[8,128,256]{2,1,0:T(8,128)(2,1)}, u32[]{:S(2)}) copy-start(bf16[8,128,256]{2,1,0:T(8,128)(2,1)} %get-tuple-element.7) | copy-start | bytes 1572868
  46.3 1.3 %copy-start = (f32[9,64,256]{2,1,0:T(8,128)S(1)}, f32[9,64,256]{2,1,0:T(8,128)}, u32[]{:S(2)}) copy-start(f32[9,64,256]{2,1,0:T(8,128)} %get-tuple-element.8) | copy-start | bytes 1769476

commit v7 on v6

--- a/solution.py
+++ b/solution.py
@@ -280,7 +280,7 @@
 
     gain = gain_ref[...]
     quarter = tile_rows // 4
-    strip = 32
+    strip = 64
 
     def convolve(b, into):
         acc = None

time: 48.6 us -> 48.6 us (level)
  no operation moved by 1% of the time
where the time goes in v7:
time: 48.6 us; the launch traced here: 48.3 us
  Pallas kernels  43.7 us (90%)
  local copies, waits for them, and re-layouts  4 us (8%)
  between operations  0.65 us (1%)
    pallas_call x1, Pallas kernels, on_device(): pl.pallas_call(functools.partial(kernel, (rows, cols, quads, split, cs, r...  43.7 us
    unnamed x7, local copies, waits for them, and re-layouts  4 us

profile of v7, /device:TPU:0, one launch (start us, length us, event | category | flops | bytes accessed | tf_op | source)
XLA Modules:
  0.0 48.3 jit_solution(4563427051304017978)
XLA Ops:
  0.6 43.7 %shard_map.67 = (bf16[8,128,256]{2,1,0:T(8,128)(2,1)}, bf16[8,128,256]{2,1,0:T(8,128)(2,1)}, f32[9,64,256]{2,1,0:T(8,128)}) custom-call(bf16[8,128,256]{2,1,0:T(8,128)(2,1)} %bitcast.14, bf16[9,64,256]{2,1,0:T(8,128)(2,1)} %bitcast.16, f32[1,256]{1,0:T(1,128)} %bitcast.17, bf16[8,128,256]{2,1,0:T(8,128)(2,1)} %bitcast.15), custom_call_target="tpu_custom_call" | custom-call | flops 3623878656 | bytes 4194304 | tf_op jit(solution)/shard_map/pallas_call | solution.py:554
  44.3 0.0 copy-start.1
  44.3 1.9 %copy.10 = bf16[1,8,128,256]{3,2,1,0:T(8,128)(2,1)} copy(bf16[1,8,128,256]{3,2,1,0:T(8,128)(2,1)} %bitcast.13) | data formatting | bytes 1048576
  46.3 0.0 copy-done.1
  46.3 0.0 copy-start
  46.3 0.8 %copy.11 = bf16[1,8,128,256]{3,2,1,0:T(8,128)(2,1)} copy(bf16[1,8,128,256]{3,2,1,0:T(8,128)(2,1)S(1)} %bitcast.12) | data formatting | bytes 1048576
  47.1 0.5 copy-done
  47.5 0.8 %copy.12 = f32[3,3,256,64]{2,3,1,0:T(8,128)} copy(f32[3,3,256,64]{2,3,1,0:T(8,128)S(1)} %bitcast.11) | data formatting | bytes 1179648
Async XLA Ops:
  44.3 1.9 %copy-start.1 = (bf16[8,128,256]{2,1,0:T(8,128)(2,1)S(1)}, bf16[8,128,256]{2,1,0:T(8,128)(2,1)}, u32[]{:S(2)}) copy-start(bf16[8,128,256]{2,1,0:T(8,128)(2,1)} %get-tuple-element.7) | copy-start | bytes 1572868
  46.3 1.3 %copy-start = (f32[9,64,256]{2,1,0:T(8,128)S(1)}, f32[9,64,256]{2,1,0:T(8,128)}, u32[]{:S(2)}) copy-start(f32[9,64,256]{2,1,0:T(8,128)} %get-tuple-element.8) | copy-start | bytes 1769476
